TPU v7x, 256 devices: a whole 4x4x8 slice. The times are simulated.
256 devices in a mesh: stn: 32 (over z, x_hi, core), chan: 8 (over y, x_lo).
Axes of the slice: x: 4 (x_hi: 2, x_lo: 2; x = x_hi * 2 + x_lo), y: 4, z: 8, core: 2. Of those that a mesh axis runs over, the one named last changes fastest.
Arguments:
- screen: float32 [64, 512, 512], P('stn'), may hold values from -6 to 6
- pierce_coords: float32 [2, 32, 8, 32, 128], P(None, 'stn', 'chan'), may hold values from 0 to 1
- query_dest: int32 [32, 8, 32, 128], P('stn', 'chan'), may hold values from 0 to 1024, as said below
- positions: float32 [3, 512], P(None, 'stn'), may hold values from -50 to 50
- directions: float32 [3, 512], replicated, may hold values from -0.7 to 0.7
- freq_ratio: float32 [256], P('chan'), may hold values from 0.7 to 1.4
- source_flux: float32 [512], replicated, may hold values from 0.2 to 5
- spectral_index: float32 [512], replicated, may hold values from -1.5 to 0.5
Outputs:
- visibilities: float32 [256, 2, 512, 512], P('chan', None, 'stn')
Inputs may be any that keep to these rules, and one draw needn't show every extreme that they name: `query_dest`: in each block every number 0 to 1023 appears in exactly one slot and empty slots hold 1024; an owner's live slots come first in its row; one owner, the same for every block, has all 128 of its slots live in every block.
All inputs are finite; a program needn't handle non-finite values.
Results may differ from a plain program's by a relative error of at most 0.008.
Values may be sent and summed in bfloat16 or wider, within the bound.
A program may use at most 128 MiB of HBM per device.

v0:
```python
import math

import jax
import jax.numpy as jnp
from jax import lax
from jax.sharding import PartitionSpec as P

TWO_PI = 2.0 * math.pi


def interpolate(values, coords, strip_rows, tile_cols):
    row_pos = coords[0] * (strip_rows - 1)
    col_pos = coords[1] * (tile_cols - 1)
    row_low = jnp.clip(jnp.floor(row_pos), 0.0, strip_rows - 2.0)
    col_low = jnp.clip(jnp.floor(col_pos), 0.0, tile_cols - 2.0)
    frac_y = row_pos - row_low
    frac_x = col_pos - col_low
    corner = row_low.astype(jnp.int32) * tile_cols + col_low.astype(jnp.int32)
    lower_pair = (1.0 - frac_x) * values[corner] + frac_x * values[corner + 1]
    upper_pair = (1.0 - frac_x) * values[corner + tile_cols] + frac_x * values[
        corner + tile_cols + 1
    ]
    return (1.0 - frac_y) * lower_pair + frac_y * upper_pair


def make_phasors(station_rows, iono_rows, directions, freq_ratio):
    delays = (
        station_rows[:, 0:1] * directions[0][None, :]
        + station_rows[:, 1:2] * directions[1][None, :]
    )
    delays = delays + station_rows[:, 2:3] * directions[2][None, :]
    angles = (TWO_PI * freq_ratio)[None, :, None] * delays[:, None, :] + iono_rows[
        :, None, :
    ] / freq_ratio[None, :, None]
    return jnp.concatenate([jnp.cos(angles), jnp.sin(angles)], axis=-1).astype(jnp.bfloat16)


def spectrum(source_flux, spectral_index, freq_ratio, count):
    return (
        source_flux[None, :]
        * jnp.exp(spectral_index[None, :] * jnp.log(freq_ratio)[:, None])
        / math.sqrt(count)
    )


def weight_rows(phasors, intensity):
    sources = intensity.shape[1]
    real_part = (phasors[:, :, :sources].astype(jnp.float32) * intensity[None]).astype(jnp.bfloat16)
    imag_part = (phasors[:, :, sources:].astype(jnp.float32) * intensity[None]).astype(jnp.bfloat16)
    upper_rows = jnp.concatenate([real_part, imag_part], axis=-1)
    lower_rows = jnp.concatenate([imag_part, -real_part], axis=-1)
    return jnp.concatenate([upper_rows, lower_rows], axis=0)


def body(
    screen,
    pierce_coords,
    query_dest,
    positions,
    directions,
    freq_ratio,
    source_flux,
    spectral_index,
):
    groups = lax.axis_size("stn")
    tile_cols = screen.shape[2]
    strip_rows = screen.shape[0] * screen.shape[1]
    values = screen.reshape(-1)
    capacity = query_dest.shape[3]
    coords = pierce_coords.reshape(2, groups, capacity)
    sampled = interpolate(
        values,
        lax.all_to_all(coords, "stn", split_axis=1, concat_axis=1, tiled=True),
        strip_rows,
        tile_cols,
    )
    returned = lax.all_to_all(sampled, "stn", split_axis=0, concat_axis=0, tiled=True)
    stations_local = positions.shape[1]
    local_sources = source_flux.shape[0] // lax.axis_size("chan")
    queries = stations_local * local_sources
    buffer = (
        jnp.zeros((queries + 1,), jnp.float32).at[query_dest.reshape(-1)].set(returned.reshape(-1))
    )
    own_iono = buffer[:queries].reshape(stations_local, local_sources)
    iono_phase = lax.all_gather(own_iono, "chan", axis=1, tiled=True)
    station_rows = positions.T
    own_phasors = make_phasors(station_rows, iono_phase, directions, freq_ratio)
    intensity = spectrum(source_flux, spectral_index, freq_ratio, source_flux.shape[0])
    weighted = weight_rows(own_phasors, intensity)
    total_stations = stations_local * groups
    channels = freq_ratio.shape[0]
    columns = jnp.einsum(
        "ack,nck->can",
        weighted,
        lax.all_gather(own_phasors, "stn", axis=0, tiled=True),
        preferred_element_type=jnp.float32,
    )
    visible = columns.reshape(channels, 2, stations_local, total_stations)
    first_row = lax.axis_index("stn") * stations_local
    rows_global = first_row + jnp.arange(stations_local, dtype=jnp.int32)
    cross_only = rows_global[:, None] != jnp.arange(total_stations, dtype=jnp.int32)[None, :]
    return jnp.where(cross_only[None, None], visible, jnp.zeros_like(visible))


def solution(mesh):
    in_specs = (
        P("stn", None, None),
        P(None, "stn", "chan", None, None),
        P("stn", "chan", None, None),
        P(None, "stn"),
        P(),
        P("chan"),
        P(),
        P(),
    )
    out_specs = P("chan", None, "stn", None)
    return jax.shard_map(body, mesh=mesh, in_specs=in_specs, out_specs=out_specs, check_vma=False)
```

profile of v0, /device:TPU:1, one launch (start us, length us, event | category | flops | bytes accessed | tf_op | source)
XLA Modules:
  0.0 433.8 jit_solution(1635080177208044203)
XLA Ops:
  6.5 1.4 copy.16
  7.9 12.6 %all-to-all-start = ((f32[2,32,128]{2,0,1:T(2,128)}), f32[2,32,128]{2,0,1:T(2,128)S(1)}, u32[]{:S(2)}, u32[]{:S(2)}) async-start(f32[2,32,128]{2,0,1:T(2,128)} %bitcast.85), calls=%async_computation | async-start | bytes 65536 | tf_op jit(solution)/shard_map/all_to_all | solution.py:73
  20.5 0.7 compare_select_fusion
  21.3 0.8 fusion.27
  22.1 0.7 fusion.28
  22.7 0.8 multiply_multiply_fusion
  23.5 0.8 slice_bitcast_fusion.2
  24.3 2.1 copy.14
  26.5 3.7 all-to-all-done
  30.1 0.1 multiply_add_fusion.1
  30.2 23.0 %gather_fusion = f32[4096]{0:T(1024)S(1)} fusion(f32[524288]{0:T(1024)S(1)} %bitcast.88, s32[4096]{0:T(1024)S(1)} %get-tuple-element.11), kind=kCustom, calls=%fused_computation | custom fusion | bytes 49152 | tf_op jit(solution)/shard_map/gather | solution.py:19
  53.3 23.0 %gather_fusion.1 = f32[4096]{0:T(1024)S(1)} fusion(f32[524288]{0:T(1024)S(1)} %bitcast.89, s32[4096]{0:T(1024)S(1)} %get-tuple-element.12), kind=kCustom, calls=%fused_computation.1 | custom fusion | bytes 49152 | tf_op jit(solution)/shard_map/gather | solution.py:19
  76.3 23.0 %gather_fusion.2 = f32[4096]{0:T(1024)S(1)} fusion(f32[524288]{0:T(1024)S(1)} %bitcast.90, s32[4096]{0:T(1024)S(1)} %get-tuple-element.13), kind=kCustom, calls=%fused_computation.2 | custom fusion | bytes 49152 | tf_op jit(solution)/shard_map/gather | solution.py:20
  99.4 0.0 copy-start
  99.4 23.0 %gather_fusion.3 = f32[4096]{0:T(1024)S(1)} fusion(f32[524288]{0:T(1024)S(1)} %bitcast.91, s32[4096]{0:T(1024)S(1)} %get-tuple-element.14), kind=kCustom, calls=%fused_computation.3 | custom fusion | bytes 49152 | tf_op jit(solution)/shard_map/gather | solution.py:20
  122.5 0.6 fusion.18
  123.1 6.1 %all-to-all-start.1 = ((f32[32,1,128]{2,1,0:T(1,128)}), f32[32,1,128]{2,1,0:T(1,128)S(1)}, u32[]{:S(2)}, u32[]{:S(2)}) async-start(f32[32,1,128]{2,1,0:T(1,128)} %bitcast.21), calls=%async_computation.1 | async-start | bytes 32768 | tf_op jit(solution)/shard_map/all_to_all | solution.py:77
  129.2 0.0 all-gather.3.cloned.1.call-start
  129.2 0.1 multiply_add_fusion
  129.3 9.2 %all-to-all-done.1 = f32[32,1,128]{2,1,0:T(1,128)S(1)} async-done(((f32[32,1,128]{2,1,0:T(1,128)}), f32[32,1,128]{2,1,0:T(1,128)S(1)}, u32[]{:S(2)}, u32[]{:S(2)}) %all-to-all-start.1) | async-done | bytes 16416 | tf_op jit(solution)/shard_map/all_to_all | solution.py:77
  138.5 15.5 %scatter_custom_fusion = f32[1025]{0:T(1024)S(1)} fusion(s32[4096]{0:T(1024)S(1)} %bitcast.101, f32[4096]{0:T(1024)S(1)} %bitcast.102, f32[]{:T(128)} %constant.11.clone.1), kind=kCustom, calls=%fused_computation.55 | custom fusion | bytes 4104 | tf_op jit(solution)/shard_map/scatter | solution.py:82
  154.0 0.1 reshape.419
  154.1 22.4 %all-gather = f32[8,64,16]{1,2,0:T(8,128)S(1)} all-gather(f32[1,64,16]{1,2,0:T(8,128)S(1)} %bitcast.99), channel_id=1, replica_groups=mesh['stn'=32,'chan'=8] {'chan'}, dimensions={0}, use_global_device_ids=true | all-gather | bytes 36864 | tf_op jit(solution)/shard_map/all_gather | solution.py:85
  176.5 0.1 reshape.473
  176.6 0.0 copy-done
  176.6 4.3 multiply_convert_fusion.1
  180.9 1.1 pad_maximum_fusion
  182.0 0.0 all-gather.3.cloned.1.call-update
  182.0 0.1 iota_compare_fusion
  182.1 3.9 fusion.26
  186.0 223.9 %all-gather.3.cloned.1.call-done = bf16[512,32,1024]{2,0,1:T(8,128)(2,1)} async-done(((bf16[16,32,1024]{2,0,1:T(8,128)(2,1)}), bf16[512,32,1024]{2,0,1:T(8,128)(2,1)}) %all-gather.3.cloned.1.call-update) | async-done | bytes 33554448 | tf_op jit(solution)/shard_map/all_gather | solution.py:95
  410.0 15.4 %fusion = f32[32,32,512]{2,1,0:T(8,128)S(1)} fusion(bf16[512,32,1024]{2,0,1:T(8,128)(2,1)} %all-gather.3.cloned.1.call-done, bf16[16,32,512]{2,0,1:T(8,128)(2,1)S(1)} %fusion.26, bf16[16,32,512]{2,0,1:T(8,128)(2,1)S(1)} %get-tuple-element.6, bf16[16,32,512]{2,0,1:T(8,128)(2,1)S(1)} %get-tuple-element.5), kind=kOutput, calls=%fused_computation.5 | convolution fusion | flops 1082130432 | bytes 37224448 | tf_op jit(solution)/shard_map/ack,nck->can/dot_general | solution.py:92
  425.4 1.6 broadcast_select_fusion
  (5 shorter events, 0.1 us)
Async XLA Ops:
  7.9 22.2 %all-to-all-start = ((f32[2,32,128]{2,0,1:T(2,128)}), f32[2,32,128]{2,0,1:T(2,128)S(1)}, u32[]{:S(2)}, u32[]{:S(2)}) async-start(f32[2,32,128]{2,0,1:T(2,128)} %bitcast.85), calls=%async_computation | async-start | bytes 65536 | tf_op jit(solution)/shard_map/all_to_all | solution.py:73
  99.4 77.2 %copy-start = (f32[32]{0:T(128)S(1)}, f32[32]{0:T(128)}, u32[]{:S(2)}) copy-start(f32[32]{0:T(128)} %param.13) | copy-start | bytes 388
  123.1 15.4 %all-to-all-start.1 = ((f32[32,1,128]{2,1,0:T(1,128)}), f32[32,1,128]{2,1,0:T(1,128)S(1)}, u32[]{:S(2)}, u32[]{:S(2)}) async-start(f32[32,1,128]{2,1,0:T(1,128)} %bitcast.21), calls=%async_computation.1 | async-start | bytes 32768 | tf_op jit(solution)/shard_map/all_to_all | solution.py:77
  129.2 280.8 %all-gather.3.cloned.1.call-start = ((), (), s32[]{:S(2)}) async-start(), calls=%async_computation.2 | async-start | bytes 34603008 | tf_op jit(solution)/shard_map/all_gather | solution.py:95
Sparse Core Ops, SparseCore 0:
  182.1 227.7 all-gather.2
where the time goes:
time: 434 us
  waiting for transfers between devices  237 us (55%)
  local copies, waits for them, and re-layouts  113 us (26%)
  blocking collectives  22.4 us (5%)
  starting transfers between devices  18.7 us (4%)
  matrix products  15.4 us (4%)
  other arithmetic  14 us (3%)
  between operations  13.5 us (3%)
    all_gather x1, waiting for transfers between devices, body(): lax.all_gather(own_phasors, 'stn', axis=0, tiled=True)  224 us
    gather x2, local copies, waits for them, and re-layouts, interpolate(): lower_pair = (1.0 - frac_x) * values[corner] + frac_x * values[corner + 1]  46.1 us
    gather x1, local copies, waits for them, and re-layouts, interpolate(): values[corner + tile_cols]  23 us
    gather x1, local copies, waits for them, and re-layouts, interpolate(): values[corner + tile_cols + 1]  23 us
    all_gather x1, blocking collectives, body(): iono_phase = lax.all_gather(own_iono, 'chan', axis=1, tiled=True)  22.4 us
    scatter x1, local copies, waits for them, and re-layouts, body(): jnp.zeros((queries + 1,), jnp.float32).at[query_dest.reshape(-1)]  15.5 us
    dot_general x1, matrix products, body(): jnp.einsum('ack,nck->can', weighted, lax.all_gather(own_phasors, 'stn', a...  15.4 us
    all_to_all x1, starting transfers between devices, body(): lax.all_to_all(coords, 'stn', split_axis=1, concat_axis=1, tiled=True)  12.6 us
  transfers between devices with their start and end apart: 3, of which 3 were waited for; matrix products, arithmetic and copies ran while one was open for 2% of the time, Pallas kernels for 0%

commit v1 on v0

v1 whole, which is shorter than its diff:
```python
import functools
import math

import jax
import jax.numpy as jnp
from jax import lax
from jax.experimental import pallas as pl
from jax.experimental.pallas import tpu as pltpu
from jax.sharding import PartitionSpec as P

MESH = pl.DeviceIdType.MESH
TWO_PI = 2.0 * math.pi
VMEM = pltpu.VMEM
NT = (((1,), (1,)), ((), ()))

SIN_COEFS = (4.4428679, -7.30744342, 3.59478808, -0.78437402)
COS_COEFS = (1.41420408, -6.97764206, 5.71523838, -1.72834863)


def half_turn_phasor(turns):
    r = turns - jnp.round(turns)
    u = r * r
    s = r * (SIN_COEFS[0] + u * (SIN_COEFS[1] + u * (SIN_COEFS[2] + u * SIN_COEFS[3])))
    c = COS_COEFS[0] + u * (COS_COEFS[1] + u * (COS_COEFS[2] + u * COS_COEFS[3]))
    return 1.0 - s * s, s * c


def exchange_kernel(n, msg_ref, out_ref, local_sem, send_sem, recv_sem):
    g = lax.axis_index("stn")
    c = lax.axis_index("chan")
    barrier = pltpu.get_barrier_semaphore()
    for k in range(1, n):
        pl.semaphore_signal(barrier, inc=1, device_id=(lax.rem(g + k, n), c), device_id_type=MESH)
    own = pltpu.make_async_copy(msg_ref.at[:, pl.ds(g, 1)], out_ref.at[:, pl.ds(g, 1)], local_sem)
    own.start()
    pl.semaphore_wait(barrier, n - 1)
    copies = []
    for k in range(1, n):
        to = lax.rem(g + k, n)
        copy = pltpu.make_async_remote_copy(
            src_ref=msg_ref.at[:, pl.ds(to, 1)],
            dst_ref=out_ref.at[:, pl.ds(g, 1)],
            send_sem=send_sem.at[k],
            recv_sem=recv_sem.at[k],
            device_id=(to, c),
            device_id_type=MESH,
        )
        copy.start()
        copies.append(copy)
    own.wait()
    for copy in copies:
        copy.wait()


def exchange(msg, n):
    return pl.pallas_call(
        functools.partial(exchange_kernel, n),
        out_shape=jax.ShapeDtypeStruct(msg.shape, msg.dtype),
        in_specs=[pl.BlockSpec(memory_space=VMEM)],
        out_specs=pl.BlockSpec(memory_space=VMEM),
        scratch_shapes=[
            pltpu.SemaphoreType.DMA,
            pltpu.SemaphoreType.DMA((n,)),
            pltpu.SemaphoreType.DMA((n,)),
        ],
        compiler_params=pltpu.CompilerParams(collective_id=0, has_side_effects=True),
        name="exchange",
    )(msg)


def lookup_kernel(addr_ref, frac_ref, screen_ref, out_ref, wide, stage):
    rows = screen_ref.shape[0]
    step = 64

    def widen(i, carry):
        here = pl.ds(pl.multiple_of(i * step, step), step)
        lane = lax.broadcasted_iota(jnp.int32, (step, 128), 1)
        tiles = [screen_ref[here, m * 128 : (m + 1) * 128] for m in range(4)]
        wide[here, :] = tiles[0]
        for b in range(1, 5):
            mixed = tiles[3] if b == 4 else jnp.where(lane >= 128 - b, tiles[b - 1], tiles[b])
            wide[pl.ds(pl.multiple_of(b * rows + i * step, step), step), :] = pltpu.roll(mixed, b, 1)
        return carry

    lax.fori_loop(0, rows // step, widen, 0)
    sub = lax.broadcasted_iota(jnp.int32, (128, 128), 0).astype(jnp.float32)

    def group(g, carry):
        for j in range(128):
            a = addr_ref[g, j]
            stage[2 * j : 2 * j + 2, :] = wide[pl.ds(a, 2), :]
        low = stage[pl.ds(0, 128, stride=2), :].T
        high = stage[pl.ds(1, 128, stride=2), :].T
        fy = frac_ref[0, pl.ds(g, 1), :]
        x = frac_ref[1, pl.ds(g, 1), :]
        mixed = (1.0 - fy) * low + fy * high
        tent = jnp.maximum(1.0 - jnp.abs(sub - x), 0.0)
        out_ref[pl.ds(g, 1), :] = jnp.sum(mixed * tent, axis=0, keepdims=True)
        return carry

    lax.fori_loop(0, addr_ref.shape[0], group, 0)


def lookup(addr, frac, screen):
    rows = screen.shape[0]
    return pl.pallas_call(
        lookup_kernel,
        out_shape=jax.ShapeDtypeStruct(addr.shape, jnp.float32),
        in_specs=[
            pl.BlockSpec(memory_space=pltpu.SMEM),
            pl.BlockSpec(memory_space=VMEM),
            pl.BlockSpec(memory_space=VMEM),
        ],
        out_specs=pl.BlockSpec(memory_space=VMEM),
        scratch_shapes=[VMEM((5 * rows, 128), jnp.float32), VMEM((256, 128), jnp.float32)],
        compiler_params=pltpu.CompilerParams(vmem_limit_bytes=32 << 20),
        name="lookup",
    )(addr, frac, screen)


def phases_kernel(
    sampled_ref, dest_ref, out_ref, back, blocks, local_sem, back_send, back_recv, z_send, z_recv,
    xy_send, xy_recv, core_send, core_recv,
):
    g = lax.axis_index("stn")
    c = lax.axis_index("chan")
    n = 32
    z = g // 4
    xh = (g // 2) % 2
    core = g % 2
    sibling = g + 1 - 2 * core
    barrier = pltpu.get_barrier_semaphore()
    xy = [(h, m) for h in range(2) for m in range(8) if (h, m) != (0, 0)]

    def xy_peer(h, m):
        return (z * 4 + ((xh + h) % 2) * 2 + core, (c + m) % 8)

    for k in range(1, n):
        pl.semaphore_signal(barrier, inc=1, device_id=((g + k) % n, c), device_id_type=MESH)
    for h, m in xy:
        if m:
            pl.semaphore_signal(barrier, inc=1, device_id=xy_peer(h, m), device_id_type=MESH)
    own = pltpu.make_async_copy(sampled_ref.at[pl.ds(g, 1)], back.at[pl.ds(g, 1)], local_sem)
    own.start()
    pl.semaphore_wait(barrier, n - 1 + 14)
    returns = []
    for k in range(1, n):
        to = (g + k) % n
        copy = pltpu.make_async_remote_copy(
            src_ref=sampled_ref.at[pl.ds(to, 1)],
            dst_ref=back.at[pl.ds(g, 1)],
            send_sem=back_send.at[k],
            recv_sem=back_recv.at[k],
            device_id=(to, c),
            device_id_type=MESH,
        )
        copy.start()
        returns.append(copy)
    own.wait()
    for copy in returns:
        copy.wait_recv()

    total = jnp.zeros((24, 128), jnp.float32)
    row_id = lax.broadcasted_iota(jnp.int32, (8, 128), 0)
    lane_id = lax.broadcasted_iota(jnp.int32, (128, 128), 0)
    for j in range(0, n, 2):
        left, right = [], []
        for o in (j, j + 1):
            v = back[o : o + 1, :]
            dest = dest_ref[o : o + 1, :]
            a = (dest // 64) % 8
            b = (dest // 512) * 64 + dest % 64
            hi = v.astype(jnp.bfloat16).astype(jnp.float32)
            mid = (v - hi).astype(jnp.bfloat16).astype(jnp.float32)
            lo = v - hi - mid
            hit = row_id == a
            left.append(
                jnp.concatenate([jnp.where(hit, part, 0.0) for part in (hi, mid, lo)], axis=0)
            )
            right.append(jnp.where(lane_id == b, 1.0, 0.0))
        total = total + lax.dot_general(
            jnp.concatenate(left, axis=1).astype(jnp.bfloat16),
            jnp.concatenate(right, axis=1).astype(jnp.bfloat16),
            NT,
            preferred_element_type=jnp.float32,
        )
    mine = (total[0:8] + total[8:16] + total[16:24]) * (1.0 / TWO_PI)
    blocks[core, xh, c, z] = mine

    z_copies = []
    for k in range(1, 8):
        copy = pltpu.make_async_remote_copy(
            src_ref=blocks.at[core, xh, c, z],
            dst_ref=blocks.at[core, xh, c, z],
            send_sem=z_send.at[k],
            recv_sem=z_recv.at[k],
            device_id=(((z + k) % 8) * 4 + xh * 2 + core, c),
            device_id_type=MESH,
        )
        copy.start()
        z_copies.append(copy)
    for copy in z_copies:
        copy.wait_recv()

    xy_copies = {}
    for h, m in xy:
        copy = pltpu.make_async_remote_copy(
            src_ref=blocks.at[core, xh, c],
            dst_ref=blocks.at[core, xh, c],
            send_sem=xy_send.at[h * 8 + m],
            recv_sem=xy_recv.at[h * 8 + m],
            device_id=xy_peer(h, m),
            device_id_type=MESH,
        )
        copy.start()
        xy_copies[h, m] = copy

    core_copies = []
    for h, m in [(0, 0)] + xy:
        if (h, m) != (0, 0):
            xy_copies[h, m].wait_recv()
        block = blocks.at[core, (xh + 2 - h) % 2, (c + 8 - m) % 8]
        copy = pltpu.make_async_remote_copy(
            src_ref=block,
            dst_ref=block,
            send_sem=core_send.at[h * 8 + m],
            recv_sem=core_recv.at[h * 8 + m],
            device_id=(sibling, c),
            device_id_type=MESH,
        )
        copy.start()
        core_copies.append(copy)
    for copy in core_copies:
        copy.wait()
    for copy in returns + z_copies + list(xy_copies.values()):
        copy.wait_send()

    lane = lax.broadcasted_iota(jnp.int32, (8, 128), 1)

    def spread(zz, carry):
        for group in range(4):
            kk, hh = group % 2, group // 2
            for m in range(4):
                even = blocks[kk, hh, 2 * m, zz]
                odd = blocks[kk, hh, 2 * m + 1, zz]
                first = pl.multiple_of((zz * 4 + group) * 16, 16)
                cols = slice(m * 128, (m + 1) * 128)
                out_ref[pl.ds(first, 8), cols] = jnp.where(lane < 64, even, pltpu.roll(odd, 64, 1))
                out_ref[pl.ds(first + 8, 8), cols] = jnp.where(
                    lane < 64, pltpu.roll(even, 64, 1), odd
                )
        return carry

    lax.fori_loop(0, 8, spread, 0)


def gather_phases(sampled, dest, stations, sources):
    dma = pltpu.SemaphoreType.DMA
    return pl.pallas_call(
        phases_kernel,
        out_shape=jax.ShapeDtypeStruct((stations, sources), jnp.float32),
        in_specs=[pl.BlockSpec(memory_space=VMEM)] * 2,
        out_specs=pl.BlockSpec(memory_space=VMEM),
        scratch_shapes=[
            VMEM((32, 128), jnp.float32),
            VMEM((2, 2, 8, 8, 8, 128), jnp.float32),
            dma,
            dma((32,)), dma((32,)),
            dma((8,)), dma((8,)),
            dma((16,)), dma((16,)),
            dma((16,)), dma((16,)),
        ],
        compiler_params=pltpu.CompilerParams(
            collective_id=1, has_side_effects=True, vmem_limit_bytes=32 << 20
        ),
        name="phases",
    )(sampled, dest)


def visibility_kernel(
    msg_ref, phase_ref, directions_ref, freq_ref, flux_ref, index_ref, out_ref, delay, phasor
):
    stations, sources = phase_ref.shape
    g = lax.axis_index("stn")
    f = pl.program_id(0)
    tile = 16

    @pl.when(f == 0)
    def _():
        turned = msg_ref[2].T
        for block in range(stations // tile):
            cols = [turned[j * 16 : (j + 1) * 16, block : block + 1] for j in range(3)]
            d = (cols[0] * directions_ref[0:1, :] + cols[1] * directions_ref[1:2, :]) + cols[
                2
            ] * directions_ref[2:3, :]
            delay[block * tile : (block + 1) * tile, :] = d

    freq = freq_ref[f]
    wide = jnp.full((1, sources), freq, jnp.float32)
    inverse = 1.0 / wide
    intensity = (
        flux_ref[...] * jnp.exp(index_ref[...] * jnp.log(wide)) * (1.0 / math.sqrt(sources))
    )

    def phasors(here):
        turns = freq * delay[here, :] + inverse * phase_ref[here, :]
        return half_turn_phasor(turns)

    re, im = phasors(pl.ds(pl.multiple_of(g * 16, 16), 16))
    re = (re * intensity).astype(jnp.bfloat16)
    im = (im * intensity).astype(jnp.bfloat16)
    left = jnp.concatenate(
        [jnp.concatenate([re, im], axis=1), jnp.concatenate([im, -re], axis=1)], axis=0
    )
    rows = lax.broadcasted_iota(jnp.int32, (16, 256), 0) + g * 16
    cols = lax.broadcasted_iota(jnp.int32, (16, 256), 1)
    for part in range(stations // 256):
        for t in range(256 // tile):
            first = part * 256 + t * tile
            re, im = phasors(slice(first, first + tile))
            phasor[first : first + tile, :sources] = re.astype(jnp.bfloat16)
            phasor[first : first + tile, sources:] = im.astype(jnp.bfloat16)
        here = slice(part * 256, (part + 1) * 256)
        result = lax.dot_general(left, phasor[here, :], NT, preferred_element_type=jnp.float32)
        cross = rows != cols + part * 256
        out_ref[0, 0, :, here] = jnp.where(cross, result[:16], 0.0)
        out_ref[0, 1, :, here] = jnp.where(cross, result[16:], 0.0)


def visibilities(msg, phases, directions, freq_ratio, flux, index):
    stations, sources = phases.shape
    channels = freq_ratio.shape[0]
    vmem = pl.BlockSpec(memory_space=VMEM)
    return pl.pallas_call(
        visibility_kernel,
        grid=(channels,),
        out_shape=jax.ShapeDtypeStruct((channels, 2, 16, stations), jnp.float32),
        in_specs=[vmem, vmem, vmem, pl.BlockSpec(memory_space=pltpu.SMEM), vmem, vmem],
        out_specs=pl.BlockSpec((1, 2, 16, stations), lambda f: (f, 0, 0, 0)),
        scratch_shapes=[
            VMEM((stations, sources), jnp.float32),
            VMEM((stations, 2 * sources), jnp.bfloat16),
        ],
        compiler_params=pltpu.CompilerParams(vmem_limit_bytes=32 << 20),
        name="visibilities",
    )(msg, phases, directions, freq_ratio, flux, index)


def body(
    screen, pierce_coords, query_dest, positions, directions, freq_ratio, source_flux, spectral_index
):
    groups = lax.axis_size("stn")
    tile_cols = screen.shape[2]
    strip = screen.reshape(-1, tile_cols)
    capacity = query_dest.shape[3]
    coords = pierce_coords.reshape(2, groups, capacity)
    station_row = jnp.pad(positions.reshape(1, 1, -1), ((0, 0), (0, 0), (0, capacity - positions.size)))
    msg = jnp.concatenate(
        [coords, jnp.broadcast_to(station_row, (1, groups, capacity))], axis=0
    )
    msg = exchange(msg, groups)

    row_pos = msg[0] * (strip.shape[0] - 1)
    col_pos = msg[1] * (tile_cols - 1)
    row_low = jnp.clip(jnp.floor(row_pos), 0.0, strip.shape[0] - 2.0)
    col_low = jnp.clip(jnp.floor(col_pos), 0.0, tile_cols - 2.0)
    column = col_low.astype(jnp.int32)
    part = column // 127
    addr = part * strip.shape[0] + row_low.astype(jnp.int32)
    frac = jnp.stack([row_pos - row_low, col_pos - (part * 127).astype(jnp.float32)])
    sampled = lookup(addr, frac, strip)

    stations = positions.shape[1] * groups
    phases = gather_phases(
        sampled, query_dest.reshape(groups, capacity), stations, source_flux.shape[0]
    )
    return visibilities(
        msg, phases, directions, freq_ratio, source_flux.reshape(1, -1), spectral_index.reshape(1, -1)
    )


def solution(mesh):
    in_specs = (
        P("stn", None, None),
        P(None, "stn", "chan", None, None),
        P("stn", "chan", None, None),
        P(None, "stn"),
        P(),
        P("chan"),
        P(),
        P(),
    )
    out_specs = P("chan", None, "stn", None)
    return jax.shard_map(body, mesh=mesh, in_specs=in_specs, out_specs=out_specs, check_vma=False)
```

time: 434 us -> 96 us (0.22)
  waiting for transfers between devices: 237 us -> 0 us
  local copies, waits for them, and re-layouts: 113 us -> 2.4 us
  Pallas kernels: 0 us -> 90.1 us
  blocking collectives: 22.4 us -> 0 us
  starting transfers between devices: 18.7 us -> 0 us
  matrix products: 15.4 us -> 0 us
  between operations: 13.5 us -> 0.12 us
  other arithmetic: 14 us -> 2.95 us
    all_gather x1 -> x0, waiting for transfers between devices: 224 us -> none  [body(): lax.all_gather(own_phasors, 'stn', axis=0, tiled=True)]
    gather x4 -> x0, local copies, waits for them, and re-layouts: 92.1 us -> none  [the longest x2 46.1 us: interpolate(): lower_pair = (1.0 - frac_x) * values[corner] + frac_x * values[corner + 1]]
    pallas_call x0 -> x4, Pallas kernels: none -> 90.1 us  [the longest x1 33.1 us: visibilities(): pl.pallas_call(visibility_kernel, grid=(channels,), out_shape=jax.ShapeDt...]
    all_gather x1 -> x0, blocking collectives: 22.4 us -> none  [body(): iono_phase = lax.all_gather(own_iono, 'chan', axis=1, tiled=True)]
    all_to_all x2 -> x0, starting transfers between devices: 18.7 us -> none  [the longest x1 12.6 us: body(): lax.all_to_all(coords, 'stn', split_axis=1, concat_axis=1, tiled=True)]
    scatter x1 -> x0, local copies, waits for them, and re-layouts: 15.5 us -> none  [body(): jnp.zeros((queries + 1,), jnp.float32).at[query_dest.reshape(-1)]]
    dot_general x1 -> x0, matrix products: 15.4 us -> none  [body(): jnp.einsum('ack,nck->can', weighted, lax.all_gather(own_phasors, 'stn', a...]
    all_to_all x2 -> x0, waiting for transfers between devices: 12.8 us -> none  [the longest x1 9.15 us: body(): lax.all_to_all(sampled, 'stn', split_axis=0, concat_axis=0, tiled=True)]
  transfers between devices with their start and end apart: 3 -> 0, of which waited for: 3 -> 0; matrix products, arithmetic and copies ran while one was open for 2% -> 0% of each run, Pallas kernels for 0% -> 0%
where the time goes in v1:
time: 96 us; the launch traced here: 95.6 us
  Pallas kernels  90.1 us (94%)
  other arithmetic  2.95 us (3%)
  local copies, waits for them, and re-layouts  2.4 us (2%)
    pallas_call x1, Pallas kernels, visibilities(): pl.pallas_call(visibility_kernel, grid=(channels,), out_shape=jax.ShapeDt...  33.1 us
    pallas_call x1, Pallas kernels, gather_phases(): pl.pallas_call(phases_kernel, out_shape=jax.ShapeDtypeStruct((stations, s...  31.1 us
    pallas_call x1, Pallas kernels, exchange(): pl.pallas_call(functools.partial(exchange_kernel, n), out_shape=jax.Shape...  16.6 us
    pallas_call x1, Pallas kernels, lookup(): pl.pallas_call(lookup_kernel, out_shape=jax.ShapeDtypeStruct(addr.shape,...  9.32 us

profile of v1, /device:TPU:1, one launch (start us, length us, event | category | flops | bytes accessed | tf_op | source)
XLA Modules:
  0.0 95.6 jit_solution(7856261679344061933)
XLA Ops:
  0.0 0.0 copy-start.5
  0.0 0.0 copy-start.4
  0.0 0.0 copy-start.6
  0.0 0.0 copy-start.3
  0.0 0.0 copy-start.2
  0.0 0.8 reshape.35
  0.8 1.4 %pad_maximum_fusion.msg_ref = f32[3,32,128]{2,1,0:T(8,128)} fusion(f32[1,32,128]{2,1,0:T(8,128)S(1)} %broadcast_in_dim.8, f32[2,32,128]{2,1,0:T(8,128)} %bitcast.17), kind=kLoop, calls=%fused_computation | loop fusion | flops 12288 | bytes 98304 | tf_op jit(solution)/shard_map/concatenate | solution.py:358
  2.2 16.6 %exchange.1.msg_ref = f32[3,32,128]{2,1,0:T(8,128)} custom-call(f32[3,32,128]{2,1,0:T(8,128)} %pad_maximum_fusion.msg_ref), custom_call_target="tpu_custom_call" | custom-call | tf_op jit(solution)/shard_map/exchange/pallas_call | solution.py:56
  18.8 0.0 copy-start.1
  18.8 0.8 fusion.4
  19.7 0.8 fusion.1.addr_ref
  20.4 0.0 copy-start
  20.4 1.6 %copy-done = f32[2,512,512]{2,1,0:T(8,128)S(1)} copy-done((f32[2,512,512]{2,1,0:T(8,128)S(1)}, f32[2,512,512]{2,1,0:T(8,128)}, u32[]{:S(2)}) %copy-start) | copy-done | bytes 2097176
  22.0 9.3 %lookup.1.sampled_ref = f32[32,128]{1,0:T(8,128)S(1)} custom-call(s32[32,128]{1,0:T(8,128)S(1)} %fusion.1.addr_ref, f32[2,32,128]{2,1,0:T(8,128)S(1)} %pad_maximum_fusion.1.frac_ref, f32[1024,512]{1,0:T(8,128)S(1)} %bitcast.13), custom_call_target="tpu_custom_call" | custom-call | tf_op jit(solution)/shard_map/lookup/pallas_call | solution.py:106
  31.3 0.0 copy-done.2
  31.3 31.1 %phases.1.phase_ref = f32[512,512]{1,0:T(8,128)S(1)} custom-call(f32[32,128]{1,0:T(8,128)S(1)} %lookup.1.sampled_ref, s32[32,128]{1,0:T(8,128)S(1)} %bitcast.14), custom_call_target="tpu_custom_call" | custom-call | tf_op jit(solution)/shard_map/phases/pallas_call | solution.py:259
  62.4 0.0 copy-done.5
  62.4 0.0 copy-done.4
  62.4 0.0 copy-done.6
  62.5 0.0 copy-done.3
  62.5 0.0 copy-done.1
  62.5 33.1 %visibilities.1 = f32[32,2,16,512]{3,2,1,0:T(8,128)} custom-call(f32[3,32,128]{2,1,0:T(8,128)S(1)} %copy-done.1, f32[512,512]{1,0:T(8,128)S(1)} %phases.1.phase_ref, f32[3,512]{1,0:T(4,128)S(1)} %copy-done.3, f32[32]{0:T(128)S(1)} %copy-done.6, f32[1,512]{1,0:T(1,128)S(1)} %bitcast.15, f32[1,512]{1,0:T(1,128)S(1)} %bitcast.16), custom_call_target="tpu_custom_call" | custom-call | tf_op jit(solution)/shard_map/visibilities/pallas_call | solution.py:334
  (3 shorter events, 0.0 us)
Async XLA Ops:
  0.0 62.4 %copy-start.5 = (f32[512]{0:T(512)S(1)}, f32[512]{0:T(512)}, u32[]{:S(2)}) copy-start(f32[512]{0:T(512)} %param.15) | copy-start | bytes 6148
  0.0 62.4 %copy-start.4 = (f32[512]{0:T(512)S(1)}, f32[512]{0:T(512)}, u32[]{:S(2)}) copy-start(f32[512]{0:T(512)} %param.14) | copy-start | bytes 6148
  0.0 62.4 %copy-start.6 = (f32[32]{0:T(128)S(1)}, f32[32]{0:T(128)}, u32[]{:S(2)}) copy-start(f32[32]{0:T(128)} %freq_ref.1) | copy-start | bytes 388
  0.0 62.5 %copy-start.3 = (f32[3,512]{1,0:T(4,128)S(1)}, f32[3,512]{1,0:T(4,128)}, u32[]{:S(2)}) copy-start(f32[3,512]{1,0:T(4,128)} %directions_ref.1) | copy-start | bytes 18436
  0.0 31.3 %copy-start.2 = (s32[1,1,32,128]{3,2,1,0:T(8,128)S(1)}, s32[1,1,32,128]{3,2,1,0:T(8,128)}, u32[]{:S(2)}) copy-start(s32[1,1,32,128]{3,2,1,0:T(8,128)} %param.10) | copy-start | bytes 49156
  18.8 43.7 %copy-start.1 = (f32[3,32,128]{2,1,0:T(8,128)S(1)}, f32[3,32,128]{2,1,0:T(8,128)}, u32[]{:S(2)}) copy-start(f32[3,32,128]{2,1,0:T(8,128)} %exchange.1.msg_ref) | copy-start | bytes 147460
  20.4 1.6 %copy-start = (f32[2,512,512]{2,1,0:T(8,128)S(1)}, f32[2,512,512]{2,1,0:T(8,128)}, u32[]{:S(2)}) copy-start(f32[2,512,512]{2,1,0:T(8,128)} %param.8) | copy-start | bytes 6291460

commit v2 on v1

v2 whole, which is shorter than its diff:
```python
import functools
import math

import jax
import jax.numpy as jnp
from jax import lax
from jax.experimental import pallas as pl
from jax.experimental.pallas import tpu as pltpu
from jax.sharding import PartitionSpec as P

MESH = pl.DeviceIdType.MESH
TWO_PI = 2.0 * math.pi
VMEM = pltpu.VMEM
NT = (((1,), (1,)), ((), ()))

SIN_COEFS = (4.4428679, -7.30744342, 3.59478808, -0.78437402)
COS_COEFS = (1.41420408, -6.97764206, 5.71523838, -1.72834863)


def half_turn_phasor(turns):
    r = turns - jnp.round(turns)
    u = r * r
    s = r * (SIN_COEFS[0] + u * (SIN_COEFS[1] + u * (SIN_COEFS[2] + u * SIN_COEFS[3])))
    c = COS_COEFS[0] + u * (COS_COEFS[1] + u * (COS_COEFS[2] + u * COS_COEFS[3]))
    return 1.0 - s * s, s * c


def whole_kernel(
    coords_hbm, cells_hbm, positions_hbm, dest_hbm, directions_hbm, screen_hbm, freq_hbm, flux_hbm, index_hbm,
    out_ref,
    strip, coords_ref, msg, got, cells_ref, frac, addr_smem, wide, stage, sampled, back, blocks,
    positions_ref, dest_ref, directions_ref, freq_ref, flux_ref, index_ref,
    phase_ref, delay_ref, phasor, theirs,
    screen_sem, in_sem, local_sem, addr_sem, ask_send, ask_recv, back_send, back_recv,
    z_send, z_recv, xy_send, xy_recv, core_send, core_recv, vis_send, vis_recv,
):
    g = lax.axis_index("stn")
    c = lax.axis_index("chan")
    n = 32
    z = g // 4
    xh = (g // 2) % 2
    core = g % 2
    sibling = g + 1 - 2 * core
    rows = strip.shape[0]
    barrier = pltpu.get_barrier_semaphore()
    xy = [(h, m) for h in range(2) for m in range(8) if (h, m) != (0, 0)]

    def xy_peer(h, m):
        return (z * 4 + ((xh + h) % 2) * 2 + core, (c + m) % 8)

    def stn_peer(k):
        return ((g + k) % n, c)

    screen_copy = pltpu.make_async_copy(screen_hbm, strip, screen_sem)
    coords_copy = pltpu.make_async_copy(coords_hbm, coords_ref, in_sem.at[0])
    cells_copy = pltpu.make_async_copy(cells_hbm, msg.at[0], in_sem.at[7])
    positions_copy = pltpu.make_async_copy(positions_hbm, positions_ref, in_sem.at[1])
    later = [
        pltpu.make_async_copy(source, target, in_sem.at[2 + i])
        for i, (source, target) in enumerate(
            (
                (dest_hbm, dest_ref),
                (directions_hbm, directions_ref),
                (freq_hbm, freq_ref),
                (flux_hbm, flux_ref),
                (index_hbm, index_ref),
            )
        )
    ]
    for copy in [coords_copy, cells_copy, positions_copy, screen_copy] + later:
        copy.start()
    for k in range(1, n):
        pl.semaphore_signal(barrier, inc=1, device_id=stn_peer(k), device_id_type=MESH)
    for h, m in xy:
        if m:
            pl.semaphore_signal(barrier, inc=1, device_id=xy_peer(h, m), device_id_type=MESH)
    positions_copy.wait()
    station_row = jnp.concatenate(
        [positions_ref[j : j + 1, :] for j in range(3)] + [jnp.zeros((1, 80), jnp.float32)], axis=1
    )
    msg[3] = jnp.broadcast_to((station_row * 2.0**24).astype(jnp.int32), (n, 128))
    coords_copy.wait()
    cells_copy.wait()
    cell = msg[0]
    low_row = (cell % rows).astype(jnp.float32)
    low_col = (cell // rows * 127).astype(jnp.float32)
    msg[1] = ((coords_ref[0] * (rows - 1) - low_row) * 2.0**24).astype(jnp.int32)
    msg[2] = ((coords_ref[1] * (strip.shape[1] - 1) - low_col) * 2.0**23).astype(jnp.int32)
    own = pltpu.make_async_copy(msg.at[:, pl.ds(g, 1)], got.at[:, pl.ds(g, 1)], local_sem.at[0])
    own.start()
    pl.semaphore_wait(barrier, n - 1 + 14)

    def ask(k):
        return pltpu.make_async_remote_copy(
            src_ref=msg.at[:, pl.ds((g + k) % n, 1)],
            dst_ref=got.at[:, pl.ds(g, 1)],
            send_sem=ask_send.at[k],
            recv_sem=ask_recv.at[k],
            device_id=stn_peer(k),
            device_id_type=MESH,
        )

    for k in range(1, n):
        ask(k).start()

    screen_copy.wait()
    step = 64

    def widen(i, carry):
        here = pl.ds(pl.multiple_of(i * step, step), step)
        lane = lax.broadcasted_iota(jnp.int32, (step, 128), 1)
        tiles = [strip[here, m * 128 : (m + 1) * 128] for m in range(4)]
        wide[here, :] = tiles[0]
        for b in range(1, 5):
            mixed = tiles[3] if b == 4 else jnp.where(lane >= 128 - b, tiles[b - 1], tiles[b])
            wide[pl.ds(pl.multiple_of(b * rows + i * step, step), step), :] = pltpu.roll(mixed, b, 1)
        return carry

    lax.fori_loop(0, rows // step, widen, 0)

    for copy in later:
        copy.wait()
    own.wait()
    for k in range(1, n):
        ask(k).wait_recv()
    cells_ref[...] = jnp.clip(got[0], 0, 5 * rows - 2)
    to_smem = pltpu.make_async_copy(cells_ref, addr_smem, addr_sem)
    to_smem.start()
    frac[0] = got[1].astype(jnp.float32) * 2.0**-24
    frac[1] = got[2].astype(jnp.float32) * 2.0**-23
    to_smem.wait()

    sub = lax.broadcasted_iota(jnp.int32, (128, 128), 0).astype(jnp.float32)

    def answer(k):
        return pltpu.make_async_remote_copy(
            src_ref=sampled.at[pl.ds((g + k) % n, 1)],
            dst_ref=back.at[pl.ds(g, 1)],
            send_sem=back_send.at[k],
            recv_sem=back_recv.at[k],
            device_id=stn_peer(k),
            device_id_type=MESH,
        )

    def look_up(k, carry):
        to = (g + k) % n
        for j in range(128):
            stage[2 * j : 2 * j + 2, :] = wide[pl.ds(addr_smem[to, j], 2), :]
        low = stage[pl.ds(0, 128, stride=2), :].T
        high = stage[pl.ds(1, 128, stride=2), :].T
        fy = frac[0, pl.ds(to, 1), :]
        mixed = (1.0 - fy) * low + fy * high
        tent = jnp.maximum(1.0 - jnp.abs(sub - frac[1, pl.ds(to, 1), :]), 0.0)
        sampled[pl.ds(to, 1), :] = jnp.sum(mixed * tent, axis=0, keepdims=True)

        @pl.when(k < n)
        def _():
            answer(k).start()

        return carry

    lax.fori_loop(1, n + 1, look_up, 0)
    keep = pltpu.make_async_copy(sampled.at[pl.ds(g, 1)], back.at[pl.ds(g, 1)], local_sem.at[1])
    keep.start()
    keep.wait()
    for k in range(1, n):
        answer(k).wait_recv()

    total = jnp.zeros((24, 128), jnp.float32)
    row_id = lax.broadcasted_iota(jnp.int32, (8, 128), 0)
    lane_id = lax.broadcasted_iota(jnp.int32, (128, 128), 0)
    for j in range(0, n, 2):
        left, right = [], []
        for o in (j, j + 1):
            v = back[o : o + 1, :]
            dest = dest_ref[o : o + 1, :]
            a = (dest // 64) % 8
            b = (dest // 512) * 64 + dest % 64
            hi = v.astype(jnp.bfloat16).astype(jnp.float32)
            mid = (v - hi).astype(jnp.bfloat16).astype(jnp.float32)
            lo = v - hi - mid
            hit = row_id == a
            left.append(
                jnp.concatenate([jnp.where(hit, part, 0.0) for part in (hi, mid, lo)], axis=0)
            )
            right.append(jnp.where(lane_id == b, 1.0, 0.0))
        total = total + lax.dot_general(
            jnp.concatenate(left, axis=1).astype(jnp.bfloat16),
            jnp.concatenate(right, axis=1).astype(jnp.bfloat16),
            NT,
            preferred_element_type=jnp.float32,
        )
    mine = (total[0:8] + total[8:16] + total[16:24]) * (1.0 / TWO_PI)
    blocks[core, xh, c, z] = mine

    z_copies = []
    for k in range(1, 8):
        copy = pltpu.make_async_remote_copy(
            src_ref=blocks.at[core, xh, c, z],
            dst_ref=blocks.at[core, xh, c, z],
            send_sem=z_send.at[k],
            recv_sem=z_recv.at[k],
            device_id=(((z + k) % 8) * 4 + xh * 2 + core, c),
            device_id_type=MESH,
        )
        copy.start()
        z_copies.append(copy)

    turned = (got[3].astype(jnp.float32) * 2.0**-24).T
    for block in range(n):
        cols = [turned[j * 16 : (j + 1) * 16, block : block + 1] for j in range(3)]
        delay_ref[block * 16 : (block + 1) * 16, :] = (
            cols[0] * directions_ref[0:1, :] + cols[1] * directions_ref[1:2, :]
        ) + cols[2] * directions_ref[2:3, :]

    for copy in z_copies:
        copy.wait_recv()

    xy_copies = {}
    for h, m in xy:
        copy = pltpu.make_async_remote_copy(
            src_ref=blocks.at[core, xh, c],
            dst_ref=blocks.at[core, xh, c],
            send_sem=xy_send.at[h * 8 + m],
            recv_sem=xy_recv.at[h * 8 + m],
            device_id=xy_peer(h, m),
            device_id_type=MESH,
        )
        copy.start()
        xy_copies[h, m] = copy

    core_copies = []
    for h, m in [(0, 0)] + xy:
        if (h, m) != (0, 0):
            xy_copies[h, m].wait_recv()
        block = blocks.at[core, (xh + 2 - h) % 2, (c + 8 - m) % 8]
        copy = pltpu.make_async_remote_copy(
            src_ref=block,
            dst_ref=block,
            send_sem=core_send.at[h * 8 + m],
            recv_sem=core_recv.at[h * 8 + m],
            device_id=(sibling, c),
            device_id_type=MESH,
        )
        copy.start()
        core_copies.append(copy)
    for copy in core_copies:
        copy.wait()
    for k in range(1, n):
        ask(k).wait_send()
        answer(k).wait_send()
    for copy in z_copies + list(xy_copies.values()):
        copy.wait_send()

    lane = lax.broadcasted_iota(jnp.int32, (8, 128), 1)

    def spread(zz, carry):
        for group in range(4):
            kk, hh = group % 2, group // 2
            for m in range(4):
                even = blocks[kk, hh, 2 * m, zz]
                odd = blocks[kk, hh, 2 * m + 1, zz]
                first = pl.multiple_of((zz * 4 + group) * 16, 16)
                cols = slice(m * 128, (m + 1) * 128)
                phase_ref[pl.ds(first, 8), cols] = jnp.where(lane < 64, even, pltpu.roll(odd, 64, 1))
                phase_ref[pl.ds(first + 8, 8), cols] = jnp.where(
                    lane < 64, pltpu.roll(even, 64, 1), odd
                )
        return carry

    lax.fori_loop(0, 8, spread, 0)

    stations, sources = phase_ref.shape
    half = freq_ref.shape[0] // 2
    tile = 16
    def send(i):
        return pltpu.make_async_remote_copy(
            src_ref=theirs.at[pl.ds(2 * i, 2)],
            dst_ref=out_ref.at[pl.ds(core * half + 2 * i, 2)],
            send_sem=vis_send.at[i],
            recv_sem=vis_recv.at[i],
            device_id=(sibling, c),
            device_id_type=MESH,
        )

    def pair(i, carry):
        for which in range(2):
            f = core * half + 2 * i + which
            freq = freq_ref[f]
            wide = jnp.full((1, sources), freq, jnp.float32)
            inverse = 1.0 / wide
            intensity = (
                flux_ref[...] * jnp.exp(index_ref[...] * jnp.log(wide)) * (1.0 / math.sqrt(sources))
            )

            def phasors(here):
                return half_turn_phasor(freq * delay_ref[here, :] + inverse * phase_ref[here, :])

            upper, lower = [], []
            for group in (g, sibling):
                re, im = phasors(pl.ds(pl.multiple_of(group * 16, 16), 16))
                re = (re * intensity).astype(jnp.bfloat16)
                im = (im * intensity).astype(jnp.bfloat16)
                upper.append(jnp.concatenate([re, im], axis=1))
                lower.append(jnp.concatenate([im, -re], axis=1))
            left = jnp.concatenate(upper + lower, axis=0)
            for part in range(stations // 256):
                for t in range(256 // tile):
                    first = part * 256 + t * tile
                    re, im = phasors(slice(first, first + tile))
                    phasor[which, first : first + tile, :sources] = re.astype(jnp.bfloat16)
                    phasor[which, first : first + tile, sources:] = im.astype(jnp.bfloat16)
                here = slice(part * 256, (part + 1) * 256)
                result = lax.dot_general(
                    left, phasor[which, here, :], NT, preferred_element_type=jnp.float32
                ).astype(jnp.bfloat16)
                out_ref[f, 0, :, here] = result[0:16]
                theirs[2 * i + which, 0, :, here] = result[16:32]
                out_ref[f, 1, :, here] = result[32:48]
                theirs[2 * i + which, 1, :, here] = result[48:64]
        send(i).start()
        return carry

    lax.fori_loop(0, half // 2, pair, 0)
    for i in range(half // 2):
        send(i).wait()


def whole(coords, cells, positions, dest, directions, strip, freq, flux, index):
    dma = pltpu.SemaphoreType.DMA
    n = dest.shape[0]
    rows = strip.shape[0]
    channels = freq.shape[0]
    sources = flux.shape[1]
    stations = 16 * n
    bf16, f32 = jnp.bfloat16, jnp.float32
    return pl.pallas_call(
        whole_kernel,
        out_shape=jax.ShapeDtypeStruct((channels, 2, 16, stations), bf16),
        in_specs=[pl.BlockSpec(memory_space=pl.ANY)] * 9,
        out_specs=pl.BlockSpec(memory_space=VMEM),
        scratch_shapes=[
            VMEM(strip.shape, f32),
            VMEM((2, n, 128), f32),
            VMEM((4, n, 128), jnp.int32),
            VMEM((4, n, 128), jnp.int32),
            VMEM((n, 128), jnp.int32),
            VMEM((2, n, 128), f32),
            pltpu.SMEM((n, 128), jnp.int32),
            VMEM((5 * rows, 128), f32),
            VMEM((256, 128), f32),
            VMEM((n, 128), f32),
            VMEM((n, 128), f32),
            VMEM((2, 2, 8, 8, 8, 128), f32),
            VMEM(positions.shape, f32),
            VMEM(dest.shape, jnp.int32),
            VMEM(directions.shape, f32),
            pltpu.SMEM(freq.shape, f32),
            VMEM(flux.shape, f32),
            VMEM(index.shape, f32),
            VMEM((stations, sources), f32),
            VMEM((stations, sources), f32),
            VMEM((2, stations, 2 * sources), bf16),
            VMEM((channels // 2, 2, 16, stations), bf16),
            dma, dma((8,)), dma((2,)), dma,
            dma((32,)), dma((32,)),
            dma((33,)), dma((33,)),
            dma((8,)), dma((8,)),
            dma((16,)), dma((16,)),
            dma((16,)), dma((16,)),
            dma((channels // 4,)), dma((channels // 4,)),
        ],
        compiler_params=pltpu.CompilerParams(
            collective_id=1, has_side_effects=True, vmem_limit_bytes=60 << 20
        ),
        name="whole",
    )(coords, cells, positions, dest, directions, strip, freq, flux, index)


def body(
    screen, pierce_coords, query_dest, positions, directions, freq_ratio, source_flux, spectral_index
):
    groups = lax.axis_size("stn")
    capacity = query_dest.shape[3]
    stations = positions.shape[1] * groups
    rows = screen.shape[0] * screen.shape[1]
    cols = screen.shape[2]
    coords = pierce_coords.reshape(2, groups, capacity)
    row_low = jnp.clip(jnp.floor(coords[0] * (rows - 1)), 0.0, rows - 2.0).astype(jnp.int32)
    col_low = jnp.clip(jnp.floor(coords[1] * (cols - 1)), 0.0, cols - 2.0).astype(jnp.int32)
    visible = whole(
        coords,
        col_low // 127 * rows + row_low,
        positions,
        query_dest.reshape(groups, capacity),
        directions,
        screen.reshape(-1, screen.shape[2]),
        freq_ratio,
        source_flux.reshape(1, -1),
        spectral_index.reshape(1, -1),
    )
    own = lax.axis_index("stn") * positions.shape[1] + jnp.arange(positions.shape[1])
    cross_only = own[:, None] != jnp.arange(stations)[None, :]
    return jnp.where(cross_only[None, None], visible.astype(jnp.float32), 0.0)


def solution(mesh):
    in_specs = (
        P("stn", None, None),
        P(None, "stn", "chan", None, None),
        P("stn", "chan", None, None),
        P(None, "stn"),
        P(),
        P("chan"),
        P(),
        P(),
    )
    out_specs = P("chan", None, "stn", None)
    return jax.shard_map(body, mesh=mesh, in_specs=in_specs, out_specs=out_specs, check_vma=False)
```

time: 96 us -> 67.8 us (0.71)
  Pallas kernels: 90.1 us -> 63.2 us
  local copies, waits for them, and re-layouts: 2.4 us -> 0 us
  other arithmetic: 2.95 us -> 4.28 us
    pallas_call x4 -> x1, Pallas kernels: 90.1 us -> 63.2 us  [whole(): pl.pallas_call(whole_kernel, out_shape=jax.ShapeDtypeStruct((channels, 2,...]
    select_n x0 -> x1, other arithmetic: none -> 2.84 us  [body(): return jnp.where(cross_only[None, None], visible.astype(jnp.float32), 0.0)]
    unnamed x14 -> x0, local copies, waits for them, and re-layouts: 1.61 us -> none
    concatenate x1 -> x0, other arithmetic: 1.38 us -> none  [body(): jnp.concatenate([coords, jnp.broadcast_to(station_row, (1, groups, capaci...]
where the time goes in v2:
time: 67.8 us; the launch traced here: 67.5 us
  Pallas kernels  63.2 us (93%)
  other arithmetic  4.28 us (6%)
    pallas_call x1, Pallas kernels, whole(): pl.pallas_call(whole_kernel, out_shape=jax.ShapeDtypeStruct((channels, 2,...  63.2 us
    select_n x1, other arithmetic, body(): return jnp.where(cross_only[None, None], visible.astype(jnp.float32), 0.0)  2.84 us
    add x1, other arithmetic, body(): col_low // 127 * rows + row_low  1.36 us

profile of v2, /device:TPU:1, one launch (start us, length us, event | category | flops | bytes accessed | tf_op | source)
XLA Modules:
  0.0 67.5 jit_solution(10946074145879566726)
XLA Ops:
  0.0 0.1 iota_compare_fusion
  0.1 1.4 %fusion.1.cells_hbm = s32[32,128]{1,0:T(8,128)} fusion(f32[2,1,1,32,128]{4,3,2,1,0:T(8,128)} %param.9), kind=kLoop, calls=%fused_computation.4 | loop fusion | flops 73728 | bytes 49152 | tf_op jit(solution)/shard_map/add | solution.py:393
  1.4 63.2 %whole.1 = bf16[32,2,16,512]{3,2,1,0:T(8,128)(2,1)} custom-call(f32[2,32,128]{2,1,0:T(8,128)} %bitcast.14, s32[32,128]{1,0:T(8,128)} %fusion.1.cells_hbm, f32[3,16]{1,0:T(4,128)} %positions_hbm.1, s32[32,128]{1,0:T(8,128)} %bitcast.15, f32[3,512]{1,0:T(4,128)} %directions_hbm.1, f32[1024,512]{1,0:T(8,128)} %bitcast.13, f32[32]{0:T(128)} %freq_hbm.1, ...), custom_call_target="tpu_custom_call" | custom-call | tf_op jit(solution)/shard_map/whole/pallas_call | solution.py:337
  64.7 2.8 %convert_select_fusion = f32[32,2,16,512]{3,2,1,0:T(8,128)} fusion(bf16[32,2,16,512]{3,2,1,0:T(8,128)(2,1)} %whole.1, pred[16,512]{1,0:T(8,128)(4,1)S(1)} %iota_compare_fusion), kind=kLoop, calls=%fused_computation | loop fusion | flops 1048576 | bytes 3153920 | tf_op jit(solution)/shard_map/jit(_where)/select_n | solution.py:404
  (1 shorter events, 0.0 us)

commit v3 on v2

v3 whole, which is shorter than its diff:
```python
import functools
import math

import jax
import jax.numpy as jnp
from jax import lax
from jax.experimental import pallas as pl
from jax.experimental.pallas import tpu as pltpu
from jax.sharding import PartitionSpec as P

MESH = pl.DeviceIdType.MESH
TWO_PI = 2.0 * math.pi
VMEM = pltpu.VMEM
NT = (((1,), (1,)), ((), ()))

SIN_COEFS = (4.442852586664358, -7.306899436200296, 3.59017447630795, -0.7735545907233887)
PHASE_STEPS = 34000.0


def half_turn_phasor(turns):
    r = turns - jnp.round(turns)
    u = r * r
    s = r * (SIN_COEFS[0] + u * (SIN_COEFS[1] + u * (SIN_COEFS[2] + u * SIN_COEFS[3])))
    q = s * s
    w = jnp.maximum(2.0 - q, 1e-12)
    return 1.0 - q, s * (w * lax.rsqrt(w))


def whole_kernel(
    coords_hbm, cells_hbm, positions_hbm, dest_hbm, directions_hbm, screen_hbm, freq_hbm, flux_hbm, index_hbm,
    out_hbm,
    strip, coords_ref, msg, got, cells_ref, frac, addr_smem, wide, stage, sampled, back, blocks,
    positions_ref, dest_ref, directions_ref, freq_ref, flux_ref, index_ref,
    delays, delay, phase, phasor, intensity, inverse, total_ref,
    screen_sem, in_sem, local_sem, addr_sem, ask_send, ask_recv, back_send, back_recv,
    z_send, z_recv, xy_send, xy_recv, core_send, core_recv, vis_send, vis_recv, own_sem,
):
    g = lax.axis_index("stn")
    c = lax.axis_index("chan")
    n = 32
    z = g // 4
    xh = (g // 2) % 2
    core = g % 2
    sibling = g + 1 - 2 * core
    rows = strip.shape[0]
    barrier = pltpu.get_barrier_semaphore()
    y = c // 2
    xl = c % 2
    chip = [(0, 1), (1, 0), (1, 1)]
    xy = [(0, h, l) for h, l in chip]
    xy += [(dy, h, l) for dy in range(1, 4) for h, l in [(0, 0)] + chip]

    def xy_peer(dy, h, l):
        return (z * 4 + ((xh + h) % 2) * 2 + core, ((y + dy) % 4) * 2 + (xl + l) % 2)

    def stn_peer(k):
        return ((g + k) % n, c)

    screen_copy = pltpu.make_async_copy(screen_hbm, strip, screen_sem)
    coords_copy = pltpu.make_async_copy(coords_hbm, coords_ref, in_sem.at[0])
    cells_copy = pltpu.make_async_copy(cells_hbm, msg.at[0], in_sem.at[7])
    positions_copy = pltpu.make_async_copy(positions_hbm, positions_ref, in_sem.at[1])
    later = [
        pltpu.make_async_copy(source, target, in_sem.at[2 + i])
        for i, (source, target) in enumerate(
            (
                (dest_hbm, dest_ref),
                (directions_hbm, directions_ref),
                (freq_hbm, freq_ref),
                (flux_hbm, flux_ref),
                (index_hbm, index_ref),
            )
        )
    ]
    for copy in [coords_copy, cells_copy, positions_copy, screen_copy] + later:
        copy.start()
    for k in range(1, n):
        pl.semaphore_signal(barrier, inc=1, device_id=stn_peer(k), device_id_type=MESH)
    for dy, h, l in xy:
        if dy or l:
            pl.semaphore_signal(barrier, inc=1, device_id=xy_peer(dy, h, l), device_id_type=MESH)
    positions_copy.wait()
    station_row = jnp.concatenate(
        [positions_ref[j : j + 1, :] for j in range(3)] + [jnp.zeros((1, 80), jnp.float32)], axis=1
    )
    msg[3] = jnp.broadcast_to((station_row * 2.0**24).astype(jnp.int32), (n, 128))
    coords_copy.wait()
    cells_copy.wait()
    cell = msg[0]
    low_row = (cell % rows).astype(jnp.float32)
    low_col = (cell // rows * 127).astype(jnp.float32)
    msg[1] = ((coords_ref[0] * (rows - 1) - low_row) * 2.0**24).astype(jnp.int32)
    msg[2] = ((coords_ref[1] * (strip.shape[1] - 1) - low_col) * 2.0**23).astype(jnp.int32)
    own = pltpu.make_async_copy(msg.at[:, pl.ds(g, 1)], got.at[:, pl.ds(g, 1)], local_sem.at[0])
    own.start()
    pl.semaphore_wait(barrier, n - 1 + 14)

    def ask(k):
        return pltpu.make_async_remote_copy(
            src_ref=msg.at[:, pl.ds((g + k) % n, 1)],
            dst_ref=got.at[:, pl.ds(g, 1)],
            send_sem=ask_send.at[k],
            recv_sem=ask_recv.at[k],
            device_id=stn_peer(k),
            device_id_type=MESH,
        )

    for k in range(1, n):
        ask(k).start()

    screen_copy.wait()
    step = 64

    def widen(i, carry):
        here = pl.ds(pl.multiple_of(i * step, step), step)
        lane = lax.broadcasted_iota(jnp.int32, (step, 128), 1)
        tiles = [strip[here, m * 128 : (m + 1) * 128] for m in range(4)]
        wide[here, :] = tiles[0]
        for b in range(1, 5):
            mixed = tiles[3] if b == 4 else jnp.where(lane >= 128 - b, tiles[b - 1], tiles[b])
            wide[pl.ds(pl.multiple_of(b * rows + i * step, step), step), :] = pltpu.roll(mixed, b, 1)
        return carry

    lax.fori_loop(0, rows // step, widen, 0)

    for copy in later:
        copy.wait()
    own.wait()
    for k in range(1, n):
        ask(k).wait_recv()
    cells_ref[...] = jnp.clip(got[0], 0, 5 * rows - 2)
    to_smem = pltpu.make_async_copy(cells_ref, addr_smem, addr_sem)
    to_smem.start()
    frac[0] = got[1].astype(jnp.float32) * 2.0**-24
    frac[1] = got[2].astype(jnp.float32) * 2.0**-23
    to_smem.wait()

    sub = lax.broadcasted_iota(jnp.int32, (128, 128), 0).astype(jnp.float32)

    def answer(k):
        return pltpu.make_async_remote_copy(
            src_ref=sampled.at[pl.ds((g + k) % n, 1)],
            dst_ref=back.at[pl.ds(g, 1)],
            send_sem=back_send.at[k],
            recv_sem=back_recv.at[k],
            device_id=stn_peer(k),
            device_id_type=MESH,
        )

    batch = stage.shape[0]

    def look_up(i, carry):
        for member in range(batch):
            k = 1 + i * batch + member
            to = (g + k) % n
            for j in range(128):
                stage[member, 2 * j : 2 * j + 2, :] = wide[pl.ds(addr_smem[to, j], 2), :]
            low = stage[member, pl.ds(0, 128, stride=2), :].T
            high = stage[member, pl.ds(1, 128, stride=2), :].T
            fy = frac[0, pl.ds(to, 1), :]
            mixed = (1.0 - fy) * low + fy * high
            tent = jnp.maximum(1.0 - jnp.abs(sub - frac[1, pl.ds(to, 1), :]), 0.0)
            sampled[pl.ds(to, 1), :] = jnp.sum(mixed * tent, axis=0, keepdims=True)

        for member in range(batch):
            k = 1 + i * batch + member

            @pl.when(k < n)
            def _(k=k):
                answer(k).start()

        return carry

    lax.fori_loop(0, n // batch, look_up, 0)
    keep = pltpu.make_async_copy(sampled.at[pl.ds(g, 1)], back.at[pl.ds(g, 1)], local_sem.at[1])
    keep.start()
    keep.wait()
    for k in range(1, n):
        answer(k).wait_recv()

    total = jnp.zeros((24, 128), jnp.float32)
    row_id = lax.broadcasted_iota(jnp.int32, (8, 128), 0)
    lane_id = lax.broadcasted_iota(jnp.int32, (128, 128), 0)
    for j in range(0, n, 2):
        left, right = [], []
        for o in (j, j + 1):
            v = back[o : o + 1, :]
            dest = dest_ref[o : o + 1, :]
            a = (dest // 64) % 8
            b = (dest // 512) * 64 + dest % 64
            hi = v.astype(jnp.bfloat16).astype(jnp.float32)
            mid = (v - hi).astype(jnp.bfloat16).astype(jnp.float32)
            lo = v - hi - mid
            hit = row_id == a
            left.append(
                jnp.concatenate([jnp.where(hit, part, 0.0) for part in (hi, mid, lo)], axis=0)
            )
            right.append(jnp.where(lane_id == b, 1.0, 0.0))
        total = total + lax.dot_general(
            jnp.concatenate(left, axis=1).astype(jnp.bfloat16),
            jnp.concatenate(right, axis=1).astype(jnp.bfloat16),
            NT,
            preferred_element_type=jnp.float32,
        )
    mine = jnp.round((total[0:8] + total[8:16] + total[16:24]) * (PHASE_STEPS / TWO_PI))
    mine = mine.astype(jnp.int32)
    own_rows = pl.ds(4 * z, 4)
    blocks[y, core, xh, xl, own_rows] = (mine[0:4] << 16) | (mine[4:8] & 0xFFFF)

    z_copies = []
    for k in range(1, 8):
        copy = pltpu.make_async_remote_copy(
            src_ref=blocks.at[y, core, xh, xl, own_rows],
            dst_ref=blocks.at[y, core, xh, xl, own_rows],
            send_sem=z_send.at[k],
            recv_sem=z_recv.at[k],
            device_id=(((z + k) % 8) * 4 + xh * 2 + core, c),
            device_id_type=MESH,
        )
        copy.start()
        z_copies.append(copy)

    turned = (got[3].astype(jnp.float32) * 2.0**-24).T
    for block in range(n):
        cols = [turned[j * 16 : (j + 1) * 16, block : block + 1] for j in range(3)]
        for m in range(4):
            lanes = slice(m * 128, (m + 1) * 128)
            delays[m, block * 16 : (block + 1) * 16, :] = (
                cols[0] * directions_ref[0:1, lanes] + cols[1] * directions_ref[1:2, lanes]
            ) + cols[2] * directions_ref[2:3, lanes]
    half = freq_ref.shape[0] // 2
    sources = flux_ref.shape[0] * 128

    def prepare(i, carry):
        freq = jnp.full((8, 128), freq_ref[core * half + i], jnp.float32)
        inverse[i] = (1.0 / PHASE_STEPS) / freq
        intensity[i] = (
            flux_ref[...]
            * jnp.exp(index_ref[...] * jnp.log(freq[0:4]))
            * (1.0 / math.sqrt(sources))
        )
        total_ref[i] = jnp.zeros(total_ref.shape[1:], jnp.float32)
        return carry

    lax.fori_loop(0, half, prepare, 0)

    for copy in z_copies:
        copy.wait_recv()

    xy_copies = {}
    for dy, h, l in xy:
        copy = pltpu.make_async_remote_copy(
            src_ref=blocks.at[y, core, xh, xl],
            dst_ref=blocks.at[y, core, xh, xl],
            send_sem=xy_send.at[dy * 4 + h * 2 + l],
            recv_sem=xy_recv.at[dy * 4 + h * 2 + l],
            device_id=xy_peer(dy, h, l),
            device_id_type=MESH,
        )
        copy.start()
        xy_copies[dy, h, l] = copy

    def to_sibling(k):
        block = blocks.at[(y + 4 - k) % 4, core]
        return pltpu.make_async_remote_copy(
            src_ref=block,
            dst_ref=block,
            send_sem=core_send.at[k],
            recv_sem=core_recv.at[k],
            device_id=(sibling, c),
            device_id_type=MESH,
        )

    for h, l in chip:
        xy_copies[0, h, l].wait_recv()
    to_sibling(0).start()

    lane = lax.broadcasted_iota(jnp.int32, (8, 128), 1)
    sublane = lax.broadcasted_iota(jnp.int32, (8, 128), 0)

    def spread(k):
        to_sibling(k).wait_recv()
        m = (y + 4 - k) % 4
        delay[...] = delays[m]
        for pair in range(4):
            here = slice(pair * 8, (pair + 1) * 8)
            for group in range(4):
                kk, hh = group % 2, group // 2
                high, low = [], []
                for words in (blocks[m, kk, hh, 0, here], blocks[m, kk, hh, 1, here]):
                    high.append((words >> 16).astype(jnp.float32))
                    low.append(((words << 16) >> 16).astype(jnp.float32))
                for which in range(2):
                    even, odd = [
                        jnp.where(sublane < 4, hi, pltpu.roll(lo, 4, 0))
                        if which == 0
                        else jnp.where(sublane < 4, pltpu.roll(hi, 4, 0), lo)
                        for hi, lo in zip(high, low)
                    ]
                    first = ((2 * pair + which) * 4 + group) * 16
                    phase[first : first + 8] = jnp.where(lane < 64, even, pltpu.roll(odd, 64, 1))
                    phase[first + 8 : first + 16] = jnp.where(
                        lane < 64, pltpu.roll(even, 64, 1), odd
                    )

    stations = phase.shape[0]
    tile = 16
    chip_rows = pl.ds(pl.multiple_of((g // 2) * 32, 32), 32)

    def add_channels(k, first, count):
        m = (y + 4 - k) % 4
        for j in range(count):
            f = first + j
            freq = freq_ref[core * half + f]
            inv = inverse[f, 0:1]

            def phasors(here):
                re, im = half_turn_phasor(freq * delay[here, :] + inv * phase[here, :])
                return re.astype(jnp.bfloat16), im.astype(jnp.bfloat16)

            re, im = phasors(chip_rows)
            weight = intensity[f, pl.ds(m, 1)]
            re = (re.astype(jnp.float32) * weight).astype(jnp.bfloat16)
            im = (im.astype(jnp.float32) * weight).astype(jnp.bfloat16)
            left = jnp.concatenate(
                [jnp.concatenate([re, im], axis=1), jnp.concatenate([im, -re], axis=1)], axis=0
            )
            for t in range(stations // tile):
                here = slice(t * tile, (t + 1) * tile)
                re, im = phasors(here)
                phasor[j, here, :128] = re
                phasor[j, here, 128:] = im
            result = lax.dot_general(left, phasor[j], NT, preferred_element_type=jnp.float32)
            total_ref[f] = total_ref[f] + result.reshape(total_ref.shape[1:])

    def send(i, count):
        here = pl.ds(i * count, count)
        there = pl.ds(core * half + i * count, count)
        return (
            pltpu.make_async_copy(total_ref.at[here, :, core], out_hbm.at[there], own_sem.at[i]),
            pltpu.make_async_remote_copy(
                src_ref=total_ref.at[here, :, 1 - core],
                dst_ref=out_hbm.at[there],
                send_sem=vis_send.at[i],
                recv_sem=vis_recv.at[i],
                device_id=(sibling, c),
                device_id_type=MESH,
            ),
        )

    def finish(i, count):
        lanes = pl.ds(pl.multiple_of((g // 8) * 128, 128), 128)
        row = lax.broadcasted_iota(jnp.int32, (2, 16, 128), 0) * 16
        row = row + lax.broadcasted_iota(jnp.int32, (2, 16, 128), 1) + ((g // 2) % 4) * 32
        cross = lax.broadcasted_iota(jnp.int32, (2, 16, 128), 2) != row
        for j in range(count):
            for part in range(2):
                block = total_ref[i * count + j, part, :, :, lanes]
                total_ref[i * count + j, part, :, :, lanes] = jnp.where(cross, block, 0.0)
        for copy in send(i, count):
            copy.start()

    batch = half // 2
    quarter = half // 4

    def chunk(i, carry):
        k = i // 2

        @pl.when(i % 2 == 0)
        def _():
            spread(k)

        add_channels(k, (i % 2) * batch, batch)

        @pl.when(i == 0)
        def _():
            for dy in range(1, 4):
                for h, l in [(0, 0)] + chip:
                    xy_copies[dy, h, l].wait_recv()
                to_sibling(dy).start()

        return carry

    lax.fori_loop(0, 7, chunk, 0)
    for i in range(2):
        finish(i, quarter)

    def last(i, carry):
        add_channels(3, i * quarter, quarter)
        finish(i, quarter)
        return carry

    lax.fori_loop(2, 4, last, 0)
    for k in range(1, n):
        ask(k).wait_send()
        answer(k).wait_send()
    for copy in z_copies + list(xy_copies.values()):
        copy.wait_send()
    for k in range(4):
        to_sibling(k).wait_send()
        for copy in send(k, quarter):
            copy.wait()


def whole(coords, cells, positions, dest, directions, strip, freq, flux, index):
    dma = pltpu.SemaphoreType.DMA
    n = dest.shape[0]
    rows = strip.shape[0]
    channels = freq.shape[0]
    half = channels // 2
    stations = 16 * n
    bf16, f32 = jnp.bfloat16, jnp.float32
    return pl.pallas_call(
        whole_kernel,
        out_shape=jax.ShapeDtypeStruct((channels, 2, 16, stations), f32),
        in_specs=[pl.BlockSpec(memory_space=pl.ANY)] * 9,
        out_specs=pl.BlockSpec(memory_space=pl.ANY),
        scratch_shapes=[
            VMEM(strip.shape, f32),
            VMEM((2, n, 128), f32),
            VMEM((4, n, 128), jnp.int32),
            VMEM((4, n, 128), jnp.int32),
            VMEM((n, 128), jnp.int32),
            VMEM((2, n, 128), f32),
            pltpu.SMEM((n, 128), jnp.int32),
            VMEM((5 * rows, 128), f32),
            VMEM((4, 256, 128), f32),
            VMEM((n, 128), f32),
            VMEM((n, 128), f32),
            VMEM((4, 2, 2, 2, 32, 128), jnp.int32),
            VMEM(positions.shape, f32),
            VMEM(dest.shape, jnp.int32),
            VMEM(directions.shape, f32),
            pltpu.SMEM(freq.shape, f32),
            VMEM(flux.shape, f32),
            VMEM(index.shape, f32),
            VMEM((4, stations, 128), f32),
            VMEM((stations, 128), f32),
            VMEM((stations, 128), f32),
            VMEM((half // 2, stations, 256), bf16),
            VMEM((half, 4, 128), f32),
            VMEM((half, 8, 128), f32),
            VMEM((half, 2, 2, 16, stations), f32),
            dma, dma((8,)), dma((2,)), dma,
            dma((32,)), dma((32,)),
            dma((33,)), dma((33,)),
            dma((8,)), dma((8,)),
            dma((16,)), dma((16,)),
            dma((4,)), dma((4,)),
            dma((4,)), dma((4,)), dma((4,)),
        ],
        compiler_params=pltpu.CompilerParams(
            collective_id=1, has_side_effects=True, vmem_limit_bytes=60 << 20
        ),
        name="whole",
    )(coords, cells, positions, dest, directions, strip, freq, flux, index)


def hand_on_kernel(in_hbm, out_hbm, held, in_sem, out_sem):
    parts = in_sem.shape[0]
    size = in_hbm.shape[0] // parts
    slices = [slice(i * size, (i + 1) * size) for i in range(parts)]
    loads = [
        pltpu.make_async_copy(in_hbm.at[here], held.at[here], in_sem.at[i])
        for i, here in enumerate(slices)
    ]
    stores = [
        pltpu.make_async_copy(held.at[here], out_hbm.at[here], out_sem.at[i])
        for i, here in enumerate(slices)
    ]
    for load in loads:
        load.start()
    for load, store in zip(loads, stores):
        load.wait()
        store.start()
    for store in stores:
        store.wait()


def hand_on(x):
    return pl.pallas_call(
        hand_on_kernel,
        out_shape=jax.ShapeDtypeStruct(x.shape, x.dtype),
        in_specs=[pl.BlockSpec(memory_space=pl.ANY)],
        out_specs=pl.BlockSpec(memory_space=pl.ANY),
        scratch_shapes=[
            VMEM(x.shape, x.dtype),
            pltpu.SemaphoreType.DMA((8,)),
            pltpu.SemaphoreType.DMA((8,)),
        ],
        compiler_params=pltpu.CompilerParams(vmem_limit_bytes=60 << 20),
        name="hand_on",
    )(x)


def body(
    screen, pierce_coords, query_dest, positions, directions, freq_ratio, source_flux, spectral_index
):
    groups = lax.axis_size("stn")
    capacity = query_dest.shape[3]
    rows = screen.shape[0] * screen.shape[1]
    cols = screen.shape[2]
    coords = pierce_coords.reshape(2, groups, capacity)
    row_low = jnp.clip(jnp.floor(coords[0] * (rows - 1)), 0.0, rows - 2.0).astype(jnp.int32)
    col_low = jnp.clip(jnp.floor(coords[1] * (cols - 1)), 0.0, cols - 2.0).astype(jnp.int32)
    visible = whole(
        coords,
        col_low // 127 * rows + row_low,
        positions,
        query_dest.reshape(groups, capacity),
        directions,
        screen.reshape(rows, cols),
        freq_ratio,
        source_flux.reshape(-1, 128),
        spectral_index.reshape(-1, 128),
    )
    return hand_on(visible)


def solution(mesh):
    in_specs = (
        P("stn", None, None),
        P(None, "stn", "chan", None, None),
        P("stn", "chan", None, None),
        P(None, "stn"),
        P(),
        P("chan"),
        P(),
        P(),
    )
    out_specs = P("chan", None, "stn", None)
    return jax.shard_map(body, mesh=mesh, in_specs=in_specs, out_specs=out_specs, check_vma=False)
```

time: 67.8 us -> 59.6 us (0.88)
  Pallas kernels: 63.2 us -> 57.9 us
  other arithmetic: 4.28 us -> 1.36 us
    pallas_call x1, Pallas kernels: 63.2 us -> 55.6 us  [whole(): pl.pallas_call(whole_kernel, out_shape=jax.ShapeDtypeStruct((channels, 2,...]
    select_n x1 -> x0, other arithmetic: 2.84 us -> none  [body(): return jnp.where(cross_only[None, None], visible.astype(jnp.float32), 0.0)]
    pallas_call x0 -> x1, Pallas kernels: none -> 2.39 us  [hand_on(): pl.pallas_call(hand_on_kernel, out_shape=jax.ShapeDtypeStruct(x.shape, x....]
where the time goes in v3:
time: 59.6 us; the launch traced here: 59.3 us
  Pallas kernels  57.9 us (97%)
  other arithmetic  1.36 us (2%)
    pallas_call x1, Pallas kernels, whole(): pl.pallas_call(whole_kernel, out_shape=jax.ShapeDtypeStruct((channels, 2,...  55.6 us
    pallas_call x1, Pallas kernels, hand_on(): pl.pallas_call(hand_on_kernel, out_shape=jax.ShapeDtypeStruct(x.shape, x....  2.39 us
    add x1, other arithmetic, body(): col_low // 127 * rows + row_low  1.36 us

profile of v3, /device:TPU:1, one launch (start us, length us, event | category | flops | bytes accessed | tf_op | source)
XLA Modules:
  0.0 59.3 jit_solution(17891720135259826025)
XLA Ops:
  0.0 1.4 %fusion.1.cells_hbm = s32[32,128]{1,0:T(8,128)} fusion(f32[2,1,1,32,128]{4,3,2,1,0:T(8,128)} %param.9), kind=kLoop, calls=%fused_computation.2 | loop fusion | flops 73728 | bytes 49152 | tf_op jit(solution)/shard_map/add | solution.py:508
  1.4 55.6 %whole.1.in_hbm = f32[32,2,16,512]{3,2,1,0:T(8,128)} custom-call(f32[2,32,128]{2,1,0:T(8,128)} %bitcast.14, s32[32,128]{1,0:T(8,128)} %fusion.1.cells_hbm, f32[3,16]{1,0:T(4,128)} %positions_hbm.1, s32[32,128]{1,0:T(8,128)} %bitcast.15, f32[3,512]{1,0:T(4,128)} %directions_hbm.1, f32[1024,512]{1,0:T(8,128)} %bitcast.13, f32[32]{0:T(128)} %freq_hbm.1, ...), custom_call_target="tpu_custom_call" | custom-call | tf_op jit(solution)/shard_map/whole/pallas_call | solution.py:413
  56.9 2.4 %hand_on.1 = f32[32,2,16,512]{3,2,1,0:T(8,128)} custom-call(f32[32,2,16,512]{3,2,1,0:T(8,128)} %whole.1.in_hbm), custom_call_target="tpu_custom_call" | custom-call | tf_op jit(solution)/shard_map/hand_on/pallas_call | solution.py:481

commit v4 on v3

--- a/solution.py
+++ b/solution.py
@@ -26,20 +26,35 @@
     return 1.0 - q, s * (w * lax.rsqrt(w))
 
 
+LAYERS = (1, 7, 4, 3, 5, 2, 6, 0)
+
+
+def wrap(value, size):
+    return jnp.where(value >= size, value - size, value)
+
+
+def layer_at(i):
+    layer = LAYERS[-1]
+    for j, other in enumerate(LAYERS[:-1]):
+        layer = jnp.where(i == j, other, layer)
+    return layer
+
+
 def whole_kernel(
     coords_hbm, cells_hbm, positions_hbm, dest_hbm, directions_hbm, screen_hbm, freq_hbm, flux_hbm, index_hbm,
     out_hbm,
-    strip, coords_ref, msg, got, cells_ref, frac, addr_smem, wide, stage, sampled, back, blocks,
+    strip, coords_ref, msg, got, addr_smem, wide, stage, sampled, back, blocks,
     positions_ref, dest_ref, directions_ref, freq_ref, flux_ref, index_ref,
     delays, delay, phase, phasor, intensity, inverse, total_ref,
-    screen_sem, in_sem, local_sem, addr_sem, ask_send, ask_recv, back_send, back_recv,
+    screen_sem, in_sem, addr_sem, ask_send, ask_recv, back_send, back_recv,
     z_send, z_recv, xy_send, xy_recv, core_send, core_recv, vis_send, vis_recv, own_sem,
 ):
     g = lax.axis_index("stn")
     c = lax.axis_index("chan")
     n = 32
     z = g // 4
-    xh = (g // 2) % 2
+    sub = g % 4
+    xh = sub // 2
     core = g % 2
     sibling = g + 1 - 2 * core
     rows = strip.shape[0]
@@ -49,12 +64,13 @@
     chip = [(0, 1), (1, 0), (1, 1)]
     xy = [(0, h, l) for h, l in chip]
     xy += [(dy, h, l) for dy in range(1, 4) for h, l in [(0, 0)] + chip]
+    stn = [(dz, r) for dz in LAYERS for r in range(4) if (dz, r) != (0, 0)]
 
     def xy_peer(dy, h, l):
-        return (z * 4 + ((xh + h) % 2) * 2 + core, ((y + dy) % 4) * 2 + (xl + l) % 2)
-
-    def stn_peer(k):
-        return ((g + k) % n, c)
+        return (z * 4 + wrap(xh + h, 2) * 2 + core, wrap(y + dy, 4) * 2 + wrap(xl + l, 2))
+
+    def stn_peer(dz, r):
+        return wrap(z + dz, 8) * 4 + wrap(sub + r, 4)
 
     screen_copy = pltpu.make_async_copy(screen_hbm, strip, screen_sem)
     coords_copy = pltpu.make_async_copy(coords_hbm, coords_ref, in_sem.at[0])
@@ -74,8 +90,12 @@
     ]
     for copy in [coords_copy, cells_copy, positions_copy, screen_copy] + later:
         copy.start()
-    for k in range(1, n):
-        pl.semaphore_signal(barrier, inc=1, device_id=stn_peer(k), device_id_type=MESH)
+    for dz in (4, 3, 5, 2, 6, 1, 7, 0):
+        for r in range(4):
+            if dz or r:
+                pl.semaphore_signal(
+                    barrier, inc=1, device_id=(stn_peer(dz, r), c), device_id_type=MESH
+                )
     for dy, h, l in xy:
         if dy or l:
             pl.semaphore_signal(barrier, inc=1, device_id=xy_peer(dy, h, l), device_id_type=MESH)
@@ -86,28 +106,12 @@
     msg[3] = jnp.broadcast_to((station_row * 2.0**24).astype(jnp.int32), (n, 128))
     coords_copy.wait()
     cells_copy.wait()
-    cell = msg[0]
+    cell = jnp.clip(msg[0], 0, 5 * rows - 2)
+    msg[0] = cell
     low_row = (cell % rows).astype(jnp.float32)
     low_col = (cell // rows * 127).astype(jnp.float32)
     msg[1] = ((coords_ref[0] * (rows - 1) - low_row) * 2.0**24).astype(jnp.int32)
     msg[2] = ((coords_ref[1] * (strip.shape[1] - 1) - low_col) * 2.0**23).astype(jnp.int32)
-    own = pltpu.make_async_copy(msg.at[:, pl.ds(g, 1)], got.at[:, pl.ds(g, 1)], local_sem.at[0])
-    own.start()
-    pl.semaphore_wait(barrier, n - 1 + 14)
-
-    def ask(k):
-        return pltpu.make_async_remote_copy(
-            src_ref=msg.at[:, pl.ds((g + k) % n, 1)],
-            dst_ref=got.at[:, pl.ds(g, 1)],
-            send_sem=ask_send.at[k],
-            recv_sem=ask_recv.at[k],
-            device_id=stn_peer(k),
-            device_id_type=MESH,
-        )
-
-    for k in range(1, n):
-        ask(k).start()
-
     screen_copy.wait()
     step = 64
 
@@ -123,60 +127,84 @@
 
     lax.fori_loop(0, rows // step, widen, 0)
 
+    got[:, pl.ds(g, 1)] = msg[:, pl.ds(g, 1)]
+    pl.semaphore_wait(barrier, n - 1 + 14)
+
+    def ask(dz, r):
+        to = wrap(z + 8 - dz, 8) * 4 + wrap(sub + r, 4)
+        return pltpu.make_async_remote_copy(
+            src_ref=msg.at[:, pl.ds(to, 1)],
+            dst_ref=got.at[:, pl.ds(g, 1)],
+            send_sem=ask_send.at[dz * 4 + r],
+            recv_sem=ask_recv.at[dz * 4 + r],
+            device_id=(to, c),
+            device_id_type=MESH,
+        )
+
+    for dz, r in stn:
+        ask(dz, r).start()
     for copy in later:
         copy.wait()
-    own.wait()
-    for k in range(1, n):
-        ask(k).wait_recv()
-    cells_ref[...] = jnp.clip(got[0], 0, 5 * rows - 2)
-    to_smem = pltpu.make_async_copy(cells_ref, addr_smem, addr_sem)
-    to_smem.start()
-    frac[0] = got[1].astype(jnp.float32) * 2.0**-24
-    frac[1] = got[2].astype(jnp.float32) * 2.0**-23
-    to_smem.wait()
-
-    sub = lax.broadcasted_iota(jnp.int32, (128, 128), 0).astype(jnp.float32)
-
-    def answer(k):
+
+    def answer(dz, r):
+        to = stn_peer(dz, r)
         return pltpu.make_async_remote_copy(
-            src_ref=sampled.at[pl.ds((g + k) % n, 1)],
+            src_ref=sampled.at[pl.ds(to, 1)],
             dst_ref=back.at[pl.ds(g, 1)],
-            send_sem=back_send.at[k],
-            recv_sem=back_recv.at[k],
-            device_id=stn_peer(k),
+            send_sem=back_send.at[dz * 4 + r],
+            recv_sem=back_recv.at[dz * 4 + r],
+            device_id=(to, c),
             device_id_type=MESH,
         )
 
-    batch = stage.shape[0]
+    def cells_to_smem(dz):
+        here = pl.ds(wrap(z + dz, 8) * 4, 4)
+        return pltpu.make_async_copy(got.at[0, here], addr_smem.at[here], addr_sem.at[dz])
+
+    def receive(dz):
+        @pl.when(dz != 0)
+        def _():
+            ask(dz, 0).wait_recv()
+
+        for r in range(1, 4):
+            ask(dz, r).wait_recv()
+        cells_to_smem(dz).start()
+
+    depth = lax.broadcasted_iota(jnp.int32, (128, 128), 0).astype(jnp.float32)
+    receive(LAYERS[0])
 
     def look_up(i, carry):
-        for member in range(batch):
-            k = 1 + i * batch + member
-            to = (g + k) % n
+        dz = layer_at(i)
+
+        @pl.when(i < 7)
+        def _():
+            receive(layer_at(i + 1))
+
+        cells_to_smem(dz).wait()
+        for r in range(4):
+            to = stn_peer(dz, r)
             for j in range(128):
-                stage[member, 2 * j : 2 * j + 2, :] = wide[pl.ds(addr_smem[to, j], 2), :]
-            low = stage[member, pl.ds(0, 128, stride=2), :].T
-            high = stage[member, pl.ds(1, 128, stride=2), :].T
-            fy = frac[0, pl.ds(to, 1), :]
+                stage[r, 2 * j : 2 * j + 2, :] = wide[pl.ds(addr_smem[to, j], 2), :]
+            low = stage[r, pl.ds(0, 128, stride=2), :].T
+            high = stage[r, pl.ds(1, 128, stride=2), :].T
+            fy = got[1, pl.ds(to, 1), :].astype(jnp.float32) * 2.0**-24
+            x = got[2, pl.ds(to, 1), :].astype(jnp.float32) * 2.0**-23
             mixed = (1.0 - fy) * low + fy * high
-            tent = jnp.maximum(1.0 - jnp.abs(sub - frac[1, pl.ds(to, 1), :]), 0.0)
+            tent = jnp.maximum(1.0 - jnp.abs(depth - x), 0.0)
             sampled[pl.ds(to, 1), :] = jnp.sum(mixed * tent, axis=0, keepdims=True)
 
-        for member in range(batch):
-            k = 1 + i * batch + member
-
-            @pl.when(k < n)
-            def _(k=k):
-                answer(k).start()
-
+        @pl.when(dz != 0)
+        def _():
+            answer(dz, 0).start()
+
+        for r in range(1, 4):
+            answer(dz, r).start()
         return carry
 
-    lax.fori_loop(0, n // batch, look_up, 0)
-    keep = pltpu.make_async_copy(sampled.at[pl.ds(g, 1)], back.at[pl.ds(g, 1)], local_sem.at[1])
-    keep.start()
-    keep.wait()
-    for k in range(1, n):
-        answer(k).wait_recv()
+    lax.fori_loop(0, 8, look_up, 0)
+    back[pl.ds(g, 1)] = sampled[pl.ds(g, 1)]
+    for dz, r in stn:
+        answer(dz, r).wait_recv()
 
     total = jnp.zeros((24, 128), jnp.float32)
     row_id = lax.broadcasted_iota(jnp.int32, (8, 128), 0)
@@ -208,13 +236,13 @@
     blocks[y, core, xh, xl, own_rows] = (mine[0:4] << 16) | (mine[4:8] & 0xFFFF)
 
     z_copies = []
-    for k in range(1, 8):
+    for k in (4, 3, 5, 2, 6, 1, 7):
         copy = pltpu.make_async_remote_copy(
             src_ref=blocks.at[y, core, xh, xl, own_rows],
             dst_ref=blocks.at[y, core, xh, xl, own_rows],
             send_sem=z_send.at[k],
             recv_sem=z_recv.at[k],
-            device_id=(((z + k) % 8) * 4 + xh * 2 + core, c),
+            device_id=(wrap(z + k, 8) * 4 + sub, c),
             device_id_type=MESH,
         )
         copy.start()
@@ -261,7 +289,7 @@
         xy_copies[dy, h, l] = copy
 
     def to_sibling(k):
-        block = blocks.at[(y + 4 - k) % 4, core]
+        block = blocks.at[wrap(y + 4 - k, 4), core]
         return pltpu.make_async_remote_copy(
             src_ref=block,
             dst_ref=block,
@@ -280,7 +308,7 @@
 
     def spread(k):
         to_sibling(k).wait_recv()
-        m = (y + 4 - k) % 4
+        m = wrap(y + 4 - k, 4)
         delay[...] = delays[m]
         for pair in range(4):
             here = slice(pair * 8, (pair + 1) * 8)
@@ -308,7 +336,7 @@
     chip_rows = pl.ds(pl.multiple_of((g // 2) * 32, 32), 32)
 
     def add_channels(k, first, count):
-        m = (y + 4 - k) % 4
+        m = wrap(y + 4 - k, 4)
         for j in range(count):
             f = first + j
             freq = freq_ref[core * half + f]
@@ -391,9 +419,9 @@
         return carry
 
     lax.fori_loop(2, 4, last, 0)
-    for k in range(1, n):
-        ask(k).wait_send()
-        answer(k).wait_send()
+    for dz, r in stn:
+        ask(dz, r).wait_send()
+        answer(dz, r).wait_send()
     for copy in z_copies + list(xy_copies.values()):
         copy.wait_send()
     for k in range(4):
@@ -420,8 +448,6 @@
             VMEM((2, n, 128), f32),
             VMEM((4, n, 128), jnp.int32),
             VMEM((4, n, 128), jnp.int32),
-            VMEM((n, 128), jnp.int32),
-            VMEM((2, n, 128), f32),
             pltpu.SMEM((n, 128), jnp.int32),
             VMEM((5 * rows, 128), f32),
             VMEM((4, 256, 128), f32),
@@ -441,9 +467,9 @@
             VMEM((half, 4, 128), f32),
             VMEM((half, 8, 128), f32),
             VMEM((half, 2, 2, 16, stations), f32),
-            dma, dma((8,)), dma((2,)), dma,
+            dma, dma((8,)), dma((8,)),
             dma((32,)), dma((32,)),
-            dma((33,)), dma((33,)),
+            dma((32,)), dma((32,)),
             dma((8,)), dma((8,)),
             dma((16,)), dma((16,)),
             dma((4,)), dma((4,)),

time: 59.6 us -> 57.4 us (0.963)
  Pallas kernels: 57.9 us -> 55.7 us
    pallas_call x1, Pallas kernels: 55.6 us -> 53.3 us  [whole(): pl.pallas_call(whole_kernel, out_shape=jax.ShapeDtypeStruct((channels, 2,...]
where the time goes in v4:
time: 57.4 us; the launch traced here: 57.1 us
  Pallas kernels  55.7 us (97%)
  other arithmetic  1.36 us (2%)
    pallas_call x1, Pallas kernels, whole(): pl.pallas_call(whole_kernel, out_shape=jax.ShapeDtypeStruct((channels, 2,...  53.3 us
    pallas_call x1, Pallas kernels, hand_on(): pl.pallas_call(hand_on_kernel, out_shape=jax.ShapeDtypeStruct(x.shape, x....  2.39 us
    add x1, other arithmetic, body(): col_low // 127 * rows + row_low  1.36 us

profile of v4, /device:TPU:1, one launch (start us, length us, event | category | flops | bytes accessed | tf_op | source)
XLA Modules:
  0.0 57.1 jit_solution(10176667804769655400)
XLA Ops:
  0.0 1.4 %fusion.1.cells_hbm = s32[32,128]{1,0:T(8,128)} fusion(f32[2,1,1,32,128]{4,3,2,1,0:T(8,128)} %param.9), kind=kLoop, calls=%fused_computation.2 | loop fusion | flops 73728 | bytes 49152 | tf_op jit(solution)/shard_map/add | solution.py:534
  1.4 53.3 %whole.1.in_hbm = f32[32,2,16,512]{3,2,1,0:T(8,128)} custom-call(f32[2,32,128]{2,1,0:T(8,128)} %bitcast.14, s32[32,128]{1,0:T(8,128)} %fusion.1.cells_hbm, f32[3,16]{1,0:T(4,128)} %positions_hbm.1, s32[32,128]{1,0:T(8,128)} %bitcast.15, f32[3,512]{1,0:T(4,128)} %directions_hbm.1, f32[1024,512]{1,0:T(8,128)} %bitcast.13, f32[32]{0:T(128)} %freq_hbm.1, ...), custom_call_target="tpu_custom_call" | custom-call | tf_op jit(solution)/shard_map/whole/pallas_call | solution.py:441
  54.7 2.4 %hand_on.1 = f32[32,2,16,512]{3,2,1,0:T(8,128)} custom-call(f32[32,2,16,512]{3,2,1,0:T(8,128)} %whole.1.in_hbm), custom_call_target="tpu_custom_call" | custom-call | tf_op jit(solution)/shard_map/hand_on/pallas_call | solution.py:507

commit v5 on v4

--- a/solution.py
+++ b/solution.py
@@ -22,7 +22,7 @@
     u = r * r
     s = r * (SIN_COEFS[0] + u * (SIN_COEFS[1] + u * (SIN_COEFS[2] + u * SIN_COEFS[3])))
     q = s * s
-    w = jnp.maximum(2.0 - q, 1e-12)
+    w = 2.000001 - q
     return 1.0 - q, s * (w * lax.rsqrt(w))
 
 
@@ -45,9 +45,9 @@
     out_hbm,
     strip, coords_ref, msg, got, addr_smem, wide, stage, sampled, back, blocks,
     positions_ref, dest_ref, directions_ref, freq_ref, flux_ref, index_ref,
-    delays, delay, phase, phasor, intensity, inverse, total_ref,
+    delays, turns, phase, phasor, intensity, inverse, total_ref,
     screen_sem, in_sem, addr_sem, ask_send, ask_recv, back_send, back_recv,
-    z_send, z_recv, xy_send, xy_recv, core_send, core_recv, vis_send, vis_recv, own_sem,
+    z_send, z_recv, xy_send, xy_recv, vis_send, vis_recv, own_sem,
 ):
     g = lax.axis_index("stn")
     c = lax.axis_index("chan")
@@ -233,20 +233,23 @@
     mine = jnp.round((total[0:8] + total[8:16] + total[16:24]) * (PHASE_STEPS / TWO_PI))
     mine = mine.astype(jnp.int32)
     own_rows = pl.ds(4 * z, 4)
-    blocks[y, core, xh, xl, own_rows] = (mine[0:4] << 16) | (mine[4:8] & 0xFFFF)
+    own_words = blocks.at[y, xh, xl, core, own_rows]
+    own_words[...] = (mine[0:4] << 16) | (mine[4:8] & 0xFFFF)
 
     z_copies = []
-    for k in (4, 3, 5, 2, 6, 1, 7):
-        copy = pltpu.make_async_remote_copy(
-            src_ref=blocks.at[y, core, xh, xl, own_rows],
-            dst_ref=blocks.at[y, core, xh, xl, own_rows],
-            send_sem=z_send.at[k],
-            recv_sem=z_recv.at[k],
-            device_id=(wrap(z + k, 8) * 4 + sub, c),
-            device_id_type=MESH,
-        )
-        copy.start()
-        z_copies.append(copy)
+    for k in (4, 3, 5, 2, 6, 1, 7, 0):
+        for other in range(2):
+            if k or other:
+                copy = pltpu.make_async_remote_copy(
+                    src_ref=own_words,
+                    dst_ref=own_words,
+                    send_sem=z_send.at[k * 2 + other],
+                    recv_sem=z_recv.at[k * 2 + other],
+                    device_id=(wrap(z + k, 8) * 4 + (sub + 1 - 2 * core if other else sub), c),
+                    device_id_type=MESH,
+                )
+                copy.start()
+                z_copies.append(copy)
 
     turned = (got[3].astype(jnp.float32) * 2.0**-24).T
     for block in range(n):
@@ -260,7 +263,9 @@
     sources = flux_ref.shape[0] * 128
 
     def prepare(i, carry):
-        freq = jnp.full((8, 128), freq_ref[core * half + i], jnp.float32)
+        freq = freq_ref[core * half + i]
+        turns[i] = freq * delays[...]
+        freq = jnp.full((8, 128), freq, jnp.float32)
         inverse[i] = (1.0 / PHASE_STEPS) / freq
         intensity[i] = (
             flux_ref[...]
@@ -275,47 +280,37 @@
     for copy in z_copies:
         copy.wait_recv()
 
-    xy_copies = {}
-    for dy, h, l in xy:
-        copy = pltpu.make_async_remote_copy(
-            src_ref=blocks.at[y, core, xh, xl],
-            dst_ref=blocks.at[y, core, xh, xl],
+    def pass_on(dy, h, l):
+        block = blocks.at[y, xh, xl]
+        return pltpu.make_async_remote_copy(
+            src_ref=block,
+            dst_ref=block,
             send_sem=xy_send.at[dy * 4 + h * 2 + l],
             recv_sem=xy_recv.at[dy * 4 + h * 2 + l],
             device_id=xy_peer(dy, h, l),
             device_id_type=MESH,
         )
-        copy.start()
-        xy_copies[dy, h, l] = copy
-
-    def to_sibling(k):
-        block = blocks.at[wrap(y + 4 - k, 4), core]
-        return pltpu.make_async_remote_copy(
-            src_ref=block,
-            dst_ref=block,
-            send_sem=core_send.at[k],
-            recv_sem=core_recv.at[k],
-            device_id=(sibling, c),
-            device_id_type=MESH,
-        )
-
-    for h, l in chip:
-        xy_copies[0, h, l].wait_recv()
-    to_sibling(0).start()
+
+    for dy, h, l in xy:
+        pass_on(dy, h, l).start()
 
     lane = lax.broadcasted_iota(jnp.int32, (8, 128), 1)
     sublane = lax.broadcasted_iota(jnp.int32, (8, 128), 0)
 
     def spread(k):
-        to_sibling(k).wait_recv()
+        @pl.when(k > 0)
+        def _():
+            pass_on(k, 0, 0).wait_recv()
+
+        for h, l in chip:
+            pass_on(k, h, l).wait_recv()
         m = wrap(y + 4 - k, 4)
-        delay[...] = delays[m]
         for pair in range(4):
             here = slice(pair * 8, (pair + 1) * 8)
             for group in range(4):
                 kk, hh = group % 2, group // 2
                 high, low = [], []
-                for words in (blocks[m, kk, hh, 0, here], blocks[m, kk, hh, 1, here]):
+                for words in (blocks[m, hh, 0, kk, here], blocks[m, hh, 1, kk, here]):
                     high.append((words >> 16).astype(jnp.float32))
                     low.append(((words << 16) >> 16).astype(jnp.float32))
                 for which in range(2):
@@ -339,11 +334,10 @@
         m = wrap(y + 4 - k, 4)
         for j in range(count):
             f = first + j
-            freq = freq_ref[core * half + f]
             inv = inverse[f, 0:1]
 
             def phasors(here):
-                re, im = half_turn_phasor(freq * delay[here, :] + inv * phase[here, :])
+                re, im = half_turn_phasor(turns[f, m, here, :] + inv * phase[here, :])
                 return re.astype(jnp.bfloat16), im.astype(jnp.bfloat16)
 
             re, im = phasors(chip_rows)
@@ -388,44 +382,30 @@
         for copy in send(i, count):
             copy.start()
 
-    batch = half // 2
     quarter = half // 4
 
-    def chunk(i, carry):
-        k = i // 2
-
-        @pl.when(i % 2 == 0)
-        def _():
-            spread(k)
-
-        add_channels(k, (i % 2) * batch, batch)
-
-        @pl.when(i == 0)
-        def _():
-            for dy in range(1, 4):
-                for h, l in [(0, 0)] + chip:
-                    xy_copies[dy, h, l].wait_recv()
-                to_sibling(dy).start()
-
+    def chunk(k, carry):
+        spread(k)
+        add_channels(k, 0, half)
         return carry
 
-    lax.fori_loop(0, 7, chunk, 0)
-    for i in range(2):
-        finish(i, quarter)
+    lax.fori_loop(0, 3, chunk, 0)
+    spread(3)
 
     def last(i, carry):
         add_channels(3, i * quarter, quarter)
         finish(i, quarter)
         return carry
 
-    lax.fori_loop(2, 4, last, 0)
+    lax.fori_loop(0, 4, last, 0)
     for dz, r in stn:
         ask(dz, r).wait_send()
         answer(dz, r).wait_send()
-    for copy in z_copies + list(xy_copies.values()):
+    for copy in z_copies:
         copy.wait_send()
+    for dy, h, l in xy:
+        pass_on(dy, h, l).wait_send()
     for k in range(4):
-        to_sibling(k).wait_send()
         for copy in send(k, quarter):
             copy.wait()
 
@@ -461,18 +441,17 @@
             VMEM(flux.shape, f32),
             VMEM(index.shape, f32),
             VMEM((4, stations, 128), f32),
+            VMEM((half, 4, stations, 128), f32),
             VMEM((stations, 128), f32),
-            VMEM((stations, 128), f32),
-            VMEM((half // 2, stations, 256), bf16),
+            VMEM((half, stations, 256), bf16),
             VMEM((half, 4, 128), f32),
             VMEM((half, 8, 128), f32),
             VMEM((half, 2, 2, 16, stations), f32),
             dma, dma((8,)), dma((8,)),
             dma((32,)), dma((32,)),
             dma((32,)), dma((32,)),
-            dma((8,)), dma((8,)),
             dma((16,)), dma((16,)),
-            dma((4,)), dma((4,)),
+            dma((16,)), dma((16,)),
             dma((4,)), dma((4,)), dma((4,)),
         ],
         compiler_params=pltpu.CompilerParams(

time: 57.4 us -> 56.8 us (0.990)
  no operation moved by 1% of the time
where the time goes in v5:
time: 56.8 us; the launch traced here: 56.5 us
  Pallas kernels  55.2 us (97%)
  other arithmetic  1.36 us (2%)
    pallas_call x1, Pallas kernels, whole(): pl.pallas_call(whole_kernel, out_shape=jax.ShapeDtypeStruct((channels, 2,...  52.8 us
    pallas_call x1, Pallas kernels, hand_on(): pl.pallas_call(hand_on_kernel, out_shape=jax.ShapeDtypeStruct(x.shape, x....  2.39 us
    add x1, other arithmetic, body(): col_low // 127 * rows + row_low  1.36 us

profile of v5, /device:TPU:1, one launch (start us, length us, event | category | flops | bytes accessed | tf_op | source)
XLA Modules:
  0.0 56.5 jit_solution(14173088356197266400)
XLA Ops:
  0.0 1.4 %fusion.1.cells_hbm = s32[32,128]{1,0:T(8,128)} fusion(f32[2,1,1,32,128]{4,3,2,1,0:T(8,128)} %param.9), kind=kLoop, calls=%fused_computation.2 | loop fusion | flops 73728 | bytes 49152 | tf_op jit(solution)/shard_map/add | solution.py:513
  1.4 52.8 %whole.1.in_hbm = f32[32,2,16,512]{3,2,1,0:T(8,128)} custom-call(f32[2,32,128]{2,1,0:T(8,128)} %bitcast.14, s32[32,128]{1,0:T(8,128)} %fusion.1.cells_hbm, f32[3,16]{1,0:T(4,128)} %positions_hbm.1, s32[32,128]{1,0:T(8,128)} %bitcast.15, f32[3,512]{1,0:T(4,128)} %directions_hbm.1, f32[1024,512]{1,0:T(8,128)} %bitcast.13, f32[32]{0:T(128)} %freq_hbm.1, ...), custom_call_target="tpu_custom_call" | custom-call | tf_op jit(solution)/shard_map/whole/pallas_call | solution.py:421
  54.1 2.4 %hand_on.1 = f32[32,2,16,512]{3,2,1,0:T(8,128)} custom-call(f32[32,2,16,512]{3,2,1,0:T(8,128)} %whole.1.in_hbm), custom_call_target="tpu_custom_call" | custom-call | tf_op jit(solution)/shard_map/hand_on/pallas_call | solution.py:486

commit v6 on v5

--- a/solution.py
+++ b/solution.py
@@ -41,7 +41,7 @@
 
 
 def whole_kernel(
-    coords_hbm, cells_hbm, positions_hbm, dest_hbm, directions_hbm, screen_hbm, freq_hbm, flux_hbm, index_hbm,
+    coords_hbm, positions_hbm, dest_hbm, directions_hbm, screen_hbm, freq_hbm, flux_hbm, index_hbm,
     out_hbm,
     strip, coords_ref, msg, got, addr_smem, wide, stage, sampled, back, blocks,
     positions_ref, dest_ref, directions_ref, freq_ref, flux_ref, index_ref,
@@ -74,7 +74,6 @@
 
     screen_copy = pltpu.make_async_copy(screen_hbm, strip, screen_sem)
     coords_copy = pltpu.make_async_copy(coords_hbm, coords_ref, in_sem.at[0])
-    cells_copy = pltpu.make_async_copy(cells_hbm, msg.at[0], in_sem.at[7])
     positions_copy = pltpu.make_async_copy(positions_hbm, positions_ref, in_sem.at[1])
     later = [
         pltpu.make_async_copy(source, target, in_sem.at[2 + i])
@@ -88,7 +87,7 @@
             )
         )
     ]
-    for copy in [coords_copy, cells_copy, positions_copy, screen_copy] + later:
+    for copy in [coords_copy, positions_copy, screen_copy] + later:
         copy.start()
     for dz in (4, 3, 5, 2, 6, 1, 7, 0):
         for r in range(4):
@@ -105,13 +104,15 @@
     )
     msg[3] = jnp.broadcast_to((station_row * 2.0**24).astype(jnp.int32), (n, 128))
     coords_copy.wait()
-    cells_copy.wait()
-    cell = jnp.clip(msg[0], 0, 5 * rows - 2)
-    msg[0] = cell
-    low_row = (cell % rows).astype(jnp.float32)
-    low_col = (cell // rows * 127).astype(jnp.float32)
-    msg[1] = ((coords_ref[0] * (rows - 1) - low_row) * 2.0**24).astype(jnp.int32)
-    msg[2] = ((coords_ref[1] * (strip.shape[1] - 1) - low_col) * 2.0**23).astype(jnp.int32)
+    row_pos = coords_ref[0] * (rows - 1)
+    col_pos = coords_ref[1] * (strip.shape[1] - 1)
+    row_low = jnp.clip(jnp.floor(row_pos), 0.0, rows - 2.0)
+    col_low = jnp.clip(jnp.floor(col_pos), 0.0, strip.shape[1] - 2.0)
+    column = col_low.astype(jnp.int32)
+    part = column // 127
+    msg[0] = jnp.clip(part * rows + row_low.astype(jnp.int32), 0, 5 * rows - 2)
+    msg[1] = ((row_pos - row_low) * 2.0**24).astype(jnp.int32)
+    msg[2] = ((col_pos - (part * 127).astype(jnp.float32)) * 2.0**23).astype(jnp.int32)
     screen_copy.wait()
     step = 64
 
@@ -275,7 +276,7 @@
         total_ref[i] = jnp.zeros(total_ref.shape[1:], jnp.float32)
         return carry
 
-    lax.fori_loop(0, half, prepare, 0)
+    lax.fori_loop(0, half // 2, prepare, 0)
 
     for copy in z_copies:
         copy.wait_recv()
@@ -293,6 +294,7 @@
 
     for dy, h, l in xy:
         pass_on(dy, h, l).start()
+    lax.fori_loop(half // 2, half, prepare, 0)
 
     lane = lax.broadcasted_iota(jnp.int32, (8, 128), 1)
     sublane = lax.broadcasted_iota(jnp.int32, (8, 128), 0)
@@ -410,7 +412,7 @@
             copy.wait()
 
 
-def whole(coords, cells, positions, dest, directions, strip, freq, flux, index):
+def whole(coords, positions, dest, directions, strip, freq, flux, index):
     dma = pltpu.SemaphoreType.DMA
     n = dest.shape[0]
     rows = strip.shape[0]
@@ -421,7 +423,7 @@
     return pl.pallas_call(
         whole_kernel,
         out_shape=jax.ShapeDtypeStruct((channels, 2, 16, stations), f32),
-        in_specs=[pl.BlockSpec(memory_space=pl.ANY)] * 9,
+        in_specs=[pl.BlockSpec(memory_space=pl.ANY)] * 8,
         out_specs=pl.BlockSpec(memory_space=pl.ANY),
         scratch_shapes=[
             VMEM(strip.shape, f32),
@@ -458,7 +460,7 @@
             collective_id=1, has_side_effects=True, vmem_limit_bytes=60 << 20
         ),
         name="whole",
-    )(coords, cells, positions, dest, directions, strip, freq, flux, index)
+    )(coords, positions, dest, directions, strip, freq, flux, index)
 
 
 def hand_on_kernel(in_hbm, out_hbm, held, in_sem, out_sem):
@@ -490,8 +492,8 @@
         out_specs=pl.BlockSpec(memory_space=pl.ANY),
         scratch_shapes=[
             VMEM(x.shape, x.dtype),
-            pltpu.SemaphoreType.DMA((8,)),
-            pltpu.SemaphoreType.DMA((8,)),
+            pltpu.SemaphoreType.DMA((4,)),
+            pltpu.SemaphoreType.DMA((4,)),
         ],
         compiler_params=pltpu.CompilerParams(vmem_limit_bytes=60 << 20),
         name="hand_on",
@@ -506,11 +508,8 @@
     rows = screen.shape[0] * screen.shape[1]
     cols = screen.shape[2]
     coords = pierce_coords.reshape(2, groups, capacity)
-    row_low = jnp.clip(jnp.floor(coords[0] * (rows - 1)), 0.0, rows - 2.0).astype(jnp.int32)
-    col_low = jnp.clip(jnp.floor(coords[1] * (cols - 1)), 0.0, cols - 2.0).astype(jnp.int32)
     visible = whole(
         coords,
-        col_low // 127 * rows + row_low,
         positions,
         query_dest.reshape(groups, capacity),
         directions,

time: 56.8 us -> 55.3 us (0.974)
  other arithmetic: 1.36 us -> 0 us
    add x1 -> x0, other arithmetic: 1.36 us -> none  [body(): col_low // 127 * rows + row_low]
where the time goes in v6:
time: 55.3 us; the launch traced here: 55.2 us
  Pallas kernels  55.2 us (100%)
    pallas_call x1, Pallas kernels, whole(): pl.pallas_call(whole_kernel, out_shape=jax.ShapeDtypeStruct((channels, 2,...  52.7 us
    pallas_call x1, Pallas kernels, hand_on(): pl.pallas_call(hand_on_kernel, out_shape=jax.ShapeDtypeStruct(x.shape, x....  2.42 us

profile of v6, /device:TPU:1, one launch (start us, length us, event | category | flops | bytes accessed | tf_op | source)
XLA Modules:
  0.0 55.2 jit_solution(10484510581634182584)
XLA Ops:
  0.0 52.7 %whole.1.in_hbm = f32[32,2,16,512]{3,2,1,0:T(8,128)} custom-call(f32[2,32,128]{2,1,0:T(8,128)} %bitcast.6, f32[3,16]{1,0:T(4,128)} %positions_hbm.1, s32[32,128]{1,0:T(8,128)} %bitcast.7, f32[3,512]{1,0:T(4,128)} %directions_hbm.1, f32[1024,512]{1,0:T(8,128)} %bitcast.5, f32[32]{0:T(128)} %freq_hbm.1, f32[4,128]{1,0:T(4,128)} %bitcast.8, f32[4,128]{1,0:T(4,128)} %bitcast.9), custom_call_target="tpu_custom_call" | custom-call | tf_op jit(solution)/shard_map/whole/pallas_call | solution.py:423
  52.8 2.4 %hand_on.1 = f32[32,2,16,512]{3,2,1,0:T(8,128)} custom-call(f32[32,2,16,512]{3,2,1,0:T(8,128)} %whole.1.in_hbm), custom_call_target="tpu_custom_call" | custom-call | tf_op jit(solution)/shard_map/hand_on/pallas_call | solution.py:488

commit v7 on v6

--- a/solution.py
+++ b/solution.py
@@ -63,7 +63,7 @@
     xl = c % 2
     chip = [(0, 1), (1, 0), (1, 1)]
     xy = [(0, h, l) for h, l in chip]
-    xy += [(dy, h, l) for dy in range(1, 4) for h, l in [(0, 0)] + chip]
+    xy += [(dy, h, l) for dy in (1, 3, 2) for h, l in [(0, 0)] + chip]
     stn = [(dz, r) for dz in LAYERS for r in range(4) if (dz, r) != (0, 0)]
 
     def xy_peer(dy, h, l):
@@ -387,15 +387,16 @@
     quarter = half // 4
 
     def chunk(k, carry):
-        spread(k)
-        add_channels(k, 0, half)
+        dy = jnp.where(k == 2, 3, k)
+        spread(dy)
+        add_channels(dy, 0, half)
         return carry
 
     lax.fori_loop(0, 3, chunk, 0)
-    spread(3)
+    spread(2)
 
     def last(i, carry):
-        add_channels(3, i * quarter, quarter)
+        add_channels(2, i * quarter, quarter)
         finish(i, quarter)
         return carry
 

time: 55.3 us -> 54.4 us (0.984)
  Pallas kernels: 55.2 us -> 54.2 us
    pallas_call x1, Pallas kernels: 52.7 us -> 51.8 us  [whole(): pl.pallas_call(whole_kernel, out_shape=jax.ShapeDtypeStruct((channels, 2,...]
where the time goes in v7:
time: 54.4 us; the launch traced here: 54.2 us
  Pallas kernels  54.2 us (100%)
    pallas_call x1, Pallas kernels, whole(): pl.pallas_call(whole_kernel, out_shape=jax.ShapeDtypeStruct((channels, 2,...  51.8 us
    pallas_call x1, Pallas kernels, hand_on(): pl.pallas_call(hand_on_kernel, out_shape=jax.ShapeDtypeStruct(x.shape, x....  2.42 us

profile of v7, /device:TPU:1, one launch (start us, length us, event | category | flops | bytes accessed | tf_op | source)
XLA Modules:
  0.0 54.2 jit_solution(2050154588288696247)
XLA Ops:
  0.0 51.8 %whole.1.in_hbm = f32[32,2,16,512]{3,2,1,0:T(8,128)} custom-call(f32[2,32,128]{2,1,0:T(8,128)} %bitcast.6, f32[3,16]{1,0:T(4,128)} %positions_hbm.1, s32[32,128]{1,0:T(8,128)} %bitcast.7, f32[3,512]{1,0:T(4,128)} %directions_hbm.1, f32[1024,512]{1,0:T(8,128)} %bitcast.5, f32[32]{0:T(128)} %freq_hbm.1, f32[4,128]{1,0:T(4,128)} %bitcast.8, f32[4,128]{1,0:T(4,128)} %bitcast.9), custom_call_target="tpu_custom_call" | custom-call | tf_op jit(solution)/shard_map/whole/pallas_call | solution.py:424
  51.8 2.4 %hand_on.1 = f32[32,2,16,512]{3,2,1,0:T(8,128)} custom-call(f32[32,2,16,512]{3,2,1,0:T(8,128)} %whole.1.in_hbm), custom_call_target="tpu_custom_call" | custom-call | tf_op jit(solution)/shard_map/hand_on/pallas_call | solution.py:489
